TPU v7x, 32 devices: a whole 2x2x4 slice. The times are simulated.
32 devices in a mesh: head: 4 (over z), blk: 8 (over y, x, core).
Axes of the slice: x: 2, y: 2, z: 4, core: 2. Of those that a mesh axis runs over, the one named last changes fastest.
Arguments:
- hidden: bfloat16 [2, 2048, 768], P(None, ('head', 'blk')), may hold values from -6 to 6
- entity_flags: int32 [2, 2048], P(None, ('head', 'blk')), may hold values 0 or 1
- doc_lengths: int32 [2, 32], replicated, may hold values from 1 to 1024, 2048 in all within a row
- cotangent: bfloat16 [2, 2048, 768], P(None, ('head', 'blk')), may hold values from -6 to 6
- query_weight: bfloat16 [2359296], P(('head', 'blk')), may hold values from -0.375 to 0.375
- query_bias: bfloat16 [4, 768], replicated, may hold values from -4 to 4
- keyval_weight: bfloat16 [1179648], P(('head', 'blk')), may hold values from -0.375 to 0.375
- value_bias: bfloat16 [768], replicated, may hold values from -6 to 6
- output_weight: bfloat16 [589824], P(('head', 'blk')), may hold values from -0.21875 to 0.21875
- output_bias: bfloat16 [768], replicated, may hold values from -6 to 6
- first_gain: bfloat16 [768], replicated, may hold values from 0.5 to 1.5
- first_shift: bfloat16 [768], replicated, may hold values from -4 to 4
- inner_weight: bfloat16 [2359296], P(('head', 'blk')), may hold values from -0.21875 to 0.21875
- inner_bias: bfloat16 [3072], replicated, may hold values from -6 to 6
- outer_weight: bfloat16 [2359296], P(('head', 'blk')), may hold values from -0.109375 to 0.109375
- outer_bias: bfloat16 [768], replicated, may hold values from -6 to 6
- second_gain: bfloat16 [768], replicated, may hold values from 0.5 to 1.5
- second_shift: bfloat16 [768], replicated, may hold values from -4 to 4
Outputs:
- layer_output: bfloat16 [2, 2048, 768], P(None, ('head', 'blk'))
- grad_hidden: float32 [2, 2048, 768], P(None, ('head', 'blk'))
- grad_query_weight: float32 [2359296], P(('head', 'blk'))
- grad_query_bias: float32 [4, 768], replicated
- grad_keyval_weight: float32 [1179648], P(('head', 'blk'))
- grad_value_bias: float32 [768], replicated
- grad_output_weight: float32 [589824], P(('head', 'blk'))
- grad_output_bias: float32 [768], replicated
- grad_first_gain: float32 [768], replicated
- grad_first_shift: float32 [768], replicated
- grad_inner_weight: float32 [2359296], P(('head', 'blk'))
- grad_inner_bias: float32 [3072], replicated
- grad_outer_weight: float32 [2359296], P(('head', 'blk'))
- grad_outer_bias: float32 [768], replicated
- grad_second_gain: float32 [768], replicated
- grad_second_shift: float32 [768], replicated
Inputs may be any that keep to these rules, and one draw needn't show every extreme that they name: `doc_lengths`: each row holds the lengths of 32 documents that fill the sequence end to end in this order; the longest has exactly 1024 tokens. `entity_flags`: 1 marks an entity token, 0 a word token.
All inputs are finite; a program needn't handle non-finite values. No bound on the sum of `entity_flags` on one device may be relied on, other than what follows from the above.
Results may differ from a plain program's by a relative error of at most 0.023.
Values may be sent and summed in bfloat16 or wider, within the bound.
No kernel may reach another device: no remote copies, remote signals or barrier semaphores. Data moves between devices by JAX's collectives and lax.ppermute only.
A program may use at most 256 MiB of HBM per device.

v0:
```python
import math

import jax
import jax.numpy as jnp
from jax import lax
from jax.sharding import PartitionSpec as P

HEADS = 12
HD = 64


norm_eps = 1e-12


def layer_norm(values, gain, shift):
    centre = jnp.mean(values, -1, keepdims=True)
    centred = values - centre
    inverse = lax.rsqrt(jnp.mean(centred * centred, -1, keepdims=True) + norm_eps)
    normed = centred * inverse
    return (normed * gain + shift, normed, inverse)


def layer_norm_back(upstream, normed, inverse, gain):
    scaled = upstream * gain
    inward = inverse * (
        scaled
        - jnp.mean(scaled, -1, keepdims=True)
        - normed * jnp.mean(scaled * normed, -1, keepdims=True)
    )
    return (inward, jnp.sum(upstream * normed, 0), jnp.sum(upstream, 0))


def document_numbers(lengths, positions):
    bounds = jnp.cumsum(lengths)
    return jnp.sum((bounds[None, :] <= positions[:, None]).astype(jnp.int32), 1)


def widen_keys(keyvals, key_flags, head_size):
    keys_only = keyvals[..., :head_size]
    entity_share = key_flags.astype(jnp.bfloat16)[:, None, None]
    widened = jnp.concatenate([keys_only * (1 - entity_share), keys_only * entity_share], -1)
    return (widened, keyvals[..., head_size:])


def split_rows(arrays, block_rows):
    return tuple(
        (
            array_one.reshape((array_one.shape[0] // block_rows, block_rows) + array_one.shape[1:])
            for array_one in arrays
        )
    )


def fetch_attention(query_weight, keyval_weight, output_weight):
    return (
        lax.all_gather(query_weight, ("head", "blk"), axis=0, tiled=True),
        lax.all_gather(keyval_weight, ("head", "blk"), axis=0, tiled=True),
        lax.all_gather(output_weight, ("head", "blk"), axis=0, tiled=True),
    )


def fetch_feedforward(inner_weight, outer_weight):
    return (
        lax.all_gather(inner_weight, ("head", "blk"), axis=0, tiled=True),
        lax.all_gather(outer_weight, ("head", "blk"), axis=0, tiled=True),
    )


def body(
    hidden,
    entity_flags,
    doc_lengths,
    cotangent,
    query_weight,
    query_bias,
    keyval_weight,
    value_bias,
    output_weight,
    output_bias,
    first_gain,
    first_shift,
    inner_weight,
    inner_bias,
    outer_weight,
    outer_bias,
    second_gain,
    second_shift,
):
    micro_count, token_count, width = hidden.shape
    head_groups = lax.axis_size("head")
    cycle_length = lax.axis_size("blk")
    local_heads = HEADS // head_groups
    head_size = HD
    hidden_units = inner_bias.shape[0]
    group_rows = token_count * head_groups
    score_scale = 1.0 / math.sqrt(head_size)
    row_index = jnp.arange(group_rows, dtype=jnp.int32)
    group_positions = (
        row_index // token_count * (cycle_length * token_count)
        + lax.axis_index("blk") * token_count
        + row_index % token_count
    )
    group_flags = lax.all_gather(entity_flags, "head", axis=1, tiled=True)
    query_offset = query_bias.astype(jnp.float32)
    value_offset = value_bias.astype(jnp.float32)
    output_offset = output_bias.astype(jnp.float32)
    gain_first = first_gain.astype(jnp.float32)
    shift_first = first_shift.astype(jnp.float32)
    inner_offset = inner_bias.astype(jnp.float32)
    outer_offset = outer_bias.astype(jnp.float32)
    gain_second = second_gain.astype(jnp.float32)
    shift_second = second_shift.astype(jnp.float32)
    sum_query = jnp.zeros((width, 4, width), jnp.float32)
    sum_keyval = jnp.zeros((width, 2, width), jnp.float32)
    sum_output = jnp.zeros((width, width), jnp.float32)
    sum_inner = jnp.zeros((width, hidden_units), jnp.float32)
    sum_outer = jnp.zeros((hidden_units, width), jnp.float32)
    sum_qoffset = jnp.zeros((4, width), jnp.float32)
    sum_voffset = jnp.zeros((width,), jnp.float32)
    sum_ooffset = jnp.zeros((width,), jnp.float32)
    sum_gain_first = jnp.zeros((width,), jnp.float32)
    sum_shift_first = jnp.zeros((width,), jnp.float32)
    sum_ioffset = jnp.zeros((hidden_units,), jnp.float32)
    sum_uoffset = jnp.zeros((width,), jnp.float32)
    sum_gain_second = jnp.zeros((width,), jnp.float32)
    sum_shift_second = jnp.zeros((width,), jnp.float32)
    layer_outputs = []
    input_grads = []
    for micro_index in range(micro_count):
        attention_full = fetch_attention(query_weight, keyval_weight, output_weight)
        feedforward_full = fetch_feedforward(inner_weight, outer_weight)
        query_full = attention_full[0].reshape(width, 4, width)
        keyval_full = attention_full[1].reshape(width, 2, width)
        output_full = attention_full[2].reshape(width, width)
        inner_full = feedforward_full[0].reshape(width, hidden_units)
        outer_full = feedforward_full[1].reshape(hidden_units, width)
        tokens_now = hidden[micro_index]
        flags_now = entity_flags[micro_index]
        entity_mask = (flags_now == 1)[:, None]
        projected = (
            jnp.einsum("td,dke->tke", tokens_now, query_full, preferred_element_type=jnp.float32)
            + query_offset
        )
        toward_words = jnp.where(entity_mask, projected[:, 2], projected[:, 0]).reshape(
            token_count, HEADS, head_size
        )
        toward_entities = jnp.where(entity_mask, projected[:, 3], projected[:, 1]).reshape(
            token_count, HEADS, head_size
        )
        queries = jnp.concatenate([toward_words, toward_entities], -1).astype(jnp.bfloat16)
        paired = jnp.einsum(
            "td,dke->tke", tokens_now, keyval_full, preferred_element_type=jnp.float32
        )
        keys_local = paired[:, 0].reshape(token_count, HEADS, head_size)
        values_local = (paired[:, 1] + value_offset).reshape(token_count, HEADS, head_size)
        keyvals = jnp.concatenate([keys_local, values_local], -1).astype(jnp.bfloat16)
        query_heads, keyval_heads = (
            lax.all_to_all(queries, "head", split_axis=1, concat_axis=0, tiled=True),
            lax.all_to_all(keyvals, "head", split_axis=1, concat_axis=0, tiled=True),
        )
        flags_group = group_flags[micro_index]
        documents_group = document_numbers(doc_lengths[micro_index], group_positions)
        keys_wide, values_here = widen_keys(keyval_heads, flags_group, head_size)
        start_state = (
            jnp.full((local_heads, group_rows), -1e30, jnp.float32),
            jnp.zeros((local_heads, group_rows), jnp.float32),
            jnp.zeros((group_rows, local_heads, head_size), jnp.float32),
        )

        def attend_advance(carried, block_item):
            keyval_block, flag_block, document_block = block_item
            wide_block, value_block = widen_keys(keyval_block, flag_block, head_size)
            same_document = documents_group[:, None] == document_block[None, :]
            run_max, run_sum, run_context = carried
            scores = (
                jnp.einsum(
                    "qhd,khd->hqk", query_heads, wide_block, preferred_element_type=jnp.float32
                )
                * score_scale
            )
            scores = jnp.where(same_document[None], scores, -jnp.inf)
            new_max = jnp.maximum(run_max, jnp.max(scores, -1))
            factor = jnp.exp(run_max - new_max)
            weights = jnp.exp(scores - new_max[..., None])
            blended = jnp.einsum(
                "hqk,khd->qhd",
                weights.astype(jnp.bfloat16),
                value_block,
                preferred_element_type=jnp.float32,
            )
            return (
                (
                    new_max,
                    run_sum * factor + jnp.sum(weights, -1),
                    run_context * factor.T[..., None] + blended,
                ),
                None,
            )

        run_max, run_sum, run_context = lax.scan(
            attend_advance,
            start_state,
            split_rows(
                (
                    lax.all_gather(keyval_heads, "blk", axis=0, tiled=True),
                    lax.all_gather(flags_group, "blk", axis=0, tiled=True),
                    lax.all_gather(documents_group, "blk", axis=0, tiled=True),
                ),
                group_rows,
            ),
        )[0]
        log_total = run_max + jnp.log(run_sum)
        context_heads = (run_context / run_sum.T[..., None]).astype(jnp.bfloat16)
        context = lax.all_to_all(
            context_heads, "head", split_axis=0, concat_axis=1, tiled=True
        ).reshape(token_count, width)
        attended = jnp.dot(context, output_full, preferred_element_type=jnp.float32) + output_offset
        first, normed_first, inverse_first = layer_norm(
            tokens_now.astype(jnp.float32) + attended, gain_first, shift_first
        )
        first_low = first.astype(jnp.bfloat16)
        inner = jnp.dot(first_low, inner_full, preferred_element_type=jnp.float32) + inner_offset
        activated = jax.nn.gelu(inner).astype(jnp.bfloat16)
        outer = jnp.dot(activated, outer_full, preferred_element_type=jnp.float32) + outer_offset
        second, normed_second, inverse_second = layer_norm(first + outer, gain_second, shift_second)
        layer_outputs.append(second.astype(jnp.bfloat16))
        upstream = cotangent[micro_index].astype(jnp.float32)
        d_second, grad_gain_second, grad_shift_second = layer_norm_back(
            upstream, normed_second, inverse_second, gain_second
        )
        sum_gain_second = sum_gain_second + grad_gain_second
        sum_shift_second = sum_shift_second + grad_shift_second
        d_outer = d_second.astype(jnp.bfloat16)
        sum_outer = sum_outer + jnp.einsum(
            "tf,td->fd", activated, d_outer, preferred_element_type=jnp.float32
        )
        sum_uoffset = sum_uoffset + jnp.sum(d_outer, 0, dtype=jnp.float32)
        d_activated = jnp.einsum(
            "td,fd->tf", d_outer, outer_full, preferred_element_type=jnp.float32
        )
        d_inner = jax.vjp(jax.nn.gelu, inner)[1](d_activated)[0].astype(jnp.bfloat16)
        sum_inner = sum_inner + jnp.einsum(
            "td,tf->df", first_low, d_inner, preferred_element_type=jnp.float32
        )
        sum_ioffset = sum_ioffset + jnp.sum(d_inner, 0, dtype=jnp.float32)
        d_first = d_second + jnp.einsum(
            "tf,df->td", d_inner, inner_full, preferred_element_type=jnp.float32
        )
        d_sum, grad_gain_first, grad_shift_first = layer_norm_back(
            d_first, normed_first, inverse_first, gain_first
        )
        sum_gain_first = sum_gain_first + grad_gain_first
        sum_shift_first = sum_shift_first + grad_shift_first
        d_attended = d_sum.astype(jnp.bfloat16)
        sum_output = sum_output + jnp.einsum(
            "td,te->de", context, d_attended, preferred_element_type=jnp.float32
        )
        sum_ooffset = sum_ooffset + jnp.sum(d_attended, 0, dtype=jnp.float32)
        d_context = jnp.einsum(
            "te,de->td", d_attended, output_full, preferred_element_type=jnp.float32
        ).astype(jnp.bfloat16)
        d_heads = lax.all_to_all(
            d_context.reshape(token_count, HEADS, head_size),
            "head",
            split_axis=1,
            concat_axis=0,
            tiled=True,
        )
        delta = jnp.sum(d_heads.astype(jnp.float32) * context_heads.astype(jnp.float32), -1).T

        def query_advance(carried, block_item):
            keyval_block, flag_block, document_block = block_item
            wide_block, value_block = widen_keys(keyval_block, flag_block, head_size)
            same_document = documents_group[:, None] == document_block[None, :]
            scores = (
                jnp.einsum(
                    "qhd,khd->hqk", query_heads, wide_block, preferred_element_type=jnp.float32
                )
                * score_scale
            )
            scores = jnp.where(same_document[None], scores, -jnp.inf)
            probs = jnp.exp(scores - log_total[..., None])
            d_probs = jnp.einsum(
                "qhd,khd->hqk", d_heads, value_block, preferred_element_type=jnp.float32
            )
            d_scores = (probs * (d_probs - delta[..., None])).astype(jnp.bfloat16)
            return (
                carried
                + jnp.einsum(
                    "hqk,khd->qhd", d_scores, wide_block, preferred_element_type=jnp.float32
                )
                * score_scale,
                None,
            )

        d_queries = lax.scan(
            query_advance,
            jnp.zeros((group_rows, local_heads, 2 * head_size), jnp.float32),
            split_rows(
                (
                    lax.all_gather(keyval_heads, "blk", axis=0, tiled=True),
                    lax.all_gather(flags_group, "blk", axis=0, tiled=True),
                    lax.all_gather(documents_group, "blk", axis=0, tiled=True),
                ),
                group_rows,
            ),
        )[0]
        stats_total, stats_delta = (
            lax.all_gather(log_total.T, "blk", axis=0, tiled=True),
            lax.all_gather(delta.T, "blk", axis=0, tiled=True),
        )
        start_grads = (
            jnp.zeros((group_rows, local_heads, 2 * head_size), jnp.float32),
            jnp.zeros((group_rows, local_heads, head_size), jnp.float32),
        )

        def key_advance(carried, block_item):
            (query_block, dhead_block, document_block), (total_block, delta_block) = block_item
            same_document = documents_group[:, None] == document_block[None, :]
            d_wide, d_values = carried
            scores = (
                jnp.einsum(
                    "khd,qhd->hkq", keys_wide, query_block, preferred_element_type=jnp.float32
                )
                * score_scale
            )
            scores = jnp.where(same_document[None], scores, -jnp.inf)
            probs = jnp.exp(scores - total_block.T[:, None, :])
            d_values = d_values + jnp.einsum(
                "hkq,qhd->khd",
                probs.astype(jnp.bfloat16),
                dhead_block,
                preferred_element_type=jnp.float32,
            )
            d_probs = jnp.einsum(
                "khd,qhd->hkq", values_here, dhead_block, preferred_element_type=jnp.float32
            )
            d_scores = (probs * (d_probs - delta_block.T[:, None, :])).astype(jnp.bfloat16)
            d_wide = (
                d_wide
                + jnp.einsum(
                    "hkq,qhd->khd", d_scores, query_block, preferred_element_type=jnp.float32
                )
                * score_scale
            )
            return ((d_wide, d_values), None)

        block_items = (
            split_rows(
                (
                    lax.all_gather(query_heads, "blk", axis=0, tiled=True),
                    lax.all_gather(d_heads, "blk", axis=0, tiled=True),
                    lax.all_gather(documents_group, "blk", axis=0, tiled=True),
                ),
                group_rows,
            ),
            split_rows((stats_total, stats_delta), group_rows),
        )
        d_wide, d_values = lax.scan(key_advance, start_grads, block_items)[0]
        key_share = flags_group.astype(jnp.float32)[:, None, None]
        d_keys = d_wide[..., :head_size] * (1 - key_share) + d_wide[..., head_size:] * key_share
        d_keyvals = jnp.concatenate([d_keys, d_values], -1).astype(jnp.bfloat16)
        back_queries, back_keyvals = (
            lax.all_to_all(
                d_queries.astype(jnp.bfloat16), "head", split_axis=0, concat_axis=1, tiled=True
            ),
            lax.all_to_all(d_keyvals, "head", split_axis=0, concat_axis=1, tiled=True),
        )
        entity_now = flags_now.astype(jnp.bfloat16)[:, None]
        word_now = 1 - entity_now
        grad_words = back_queries[..., :head_size].reshape(token_count, width)
        grad_entities = back_queries[..., head_size:].reshape(token_count, width)
        d_projected = jnp.stack(
            [
                grad_words * word_now,
                grad_entities * word_now,
                grad_words * entity_now,
                grad_entities * entity_now,
            ],
            1,
        )
        d_paired = jnp.stack(
            [
                back_keyvals[..., :head_size].reshape(token_count, width),
                back_keyvals[..., head_size:].reshape(token_count, width),
            ],
            1,
        )
        sum_query = sum_query + jnp.einsum(
            "td,tke->dke", tokens_now, d_projected, preferred_element_type=jnp.float32
        )
        sum_qoffset = sum_qoffset + jnp.sum(d_projected, 0, dtype=jnp.float32)
        sum_keyval = sum_keyval + jnp.einsum(
            "td,tke->dke", tokens_now, d_paired, preferred_element_type=jnp.float32
        )
        sum_voffset = sum_voffset + jnp.sum(d_paired[:, 1], 0, dtype=jnp.float32)
        d_input = d_sum + jnp.einsum(
            "tke,dke->td", d_projected, query_full, preferred_element_type=jnp.float32
        )
        d_input = d_input + jnp.einsum(
            "tke,dke->td", d_paired, keyval_full, preferred_element_type=jnp.float32
        )
        input_grads.append(d_input)
    attention_sums = (
        lax.psum_scatter(sum_query.reshape(-1), ("head", "blk"), scatter_dimension=0, tiled=True),
        lax.psum_scatter(sum_keyval.reshape(-1), ("head", "blk"), scatter_dimension=0, tiled=True),
        lax.psum_scatter(sum_output.reshape(-1), ("head", "blk"), scatter_dimension=0, tiled=True),
    )
    feedforward_sums = (
        lax.psum_scatter(sum_inner.reshape(-1), ("head", "blk"), scatter_dimension=0, tiled=True),
        lax.psum_scatter(sum_outer.reshape(-1), ("head", "blk"), scatter_dimension=0, tiled=True),
    )
    vector_sums = lax.psum(
        (
            sum_qoffset,
            sum_voffset,
            sum_ooffset,
            sum_gain_first,
            sum_shift_first,
            sum_ioffset,
            sum_uoffset,
            sum_gain_second,
            sum_shift_second,
        ),
        ("head", "blk"),
    )
    return (
        jnp.stack(layer_outputs),
        jnp.stack(input_grads),
        attention_sums[0],
        vector_sums[0],
        attention_sums[1],
        vector_sums[1],
        attention_sums[2],
        vector_sums[2],
        vector_sums[3],
        vector_sums[4],
        feedforward_sums[0],
        vector_sums[5],
        feedforward_sums[1],
        vector_sums[6],
        vector_sums[7],
        vector_sums[8],
    )


def solution(mesh):
    return jax.shard_map(
        body,
        mesh=mesh,
        in_specs=(
            P(None, ("head", "blk"), None),
            P(None, ("head", "blk")),
            P(),
            P(None, ("head", "blk"), None),
            P(("head", "blk")),
            P(),
            P(("head", "blk")),
            P(),
            P(("head", "blk")),
            P(),
            P(),
            P(),
            P(("head", "blk")),
            P(),
            P(("head", "blk")),
            P(),
            P(),
            P(),
        ),
        out_specs=(
            P(None, ("head", "blk"), None),
            P(None, ("head", "blk"), None),
            P(("head", "blk")),
            P(),
            P(("head", "blk")),
            P(),
            P(("head", "blk")),
            P(),
            P(),
            P(),
            P(("head", "blk")),
            P(),
            P(("head", "blk")),
            P(),
            P(),
            P(),
        ),
        check_vma=False,
    )
```

profile of v0, /device:TPU:0, one launch (start us, length us, event | category | flops | bytes accessed | tf_op | source)
XLA Modules:
  0.0 1374.7 jit_solution(10072073061943033543)
XLA Ops:
  10.2 60.7 %all-gather.15.cloned.1.call-done = bf16[1179648]{0:T(1024)(128)(2,1)} async-done(((bf16[36864]{0:T(1024)(128)(2,1)}), bf16[1179648]{0:T(1024)(128)(2,1)}) %all-gather.15.cloned.1.call-update) | async-done | bytes 2359312 | tf_op jit(solution)/shard_map/all_gather | solution.py:57
  81.9 11.6 all_to_all.210
  95.6 10.8 all_to_all.211
  111.1 8.8 all-gather.3
  119.9 8.9 all-gather.1
  130.1 8.0 all-gather
  140.1 8.7 all-gather.4
  148.8 8.0 all-gather.2
  164.7 28.5 %all-gather.19.cloned.1.call-done = bf16[2359296]{0:T(1024)(128)(2,1)} async-done(((bf16[73728]{0:T(1024)(128)(2,1)}), bf16[2359296]{0:T(1024)(128)(2,1)}) %all-gather.19.cloned.1.call-update) | async-done | bytes 4718608 | tf_op jit(solution)/shard_map/all_gather | solution.py:56
  193.2 9.4 reshape.886
  232.9 14.6 %all-gather.17.cloned.1.call-done = bf16[2048,3,128]{2,0,1:T(8,128)(2,1)} async-done(((bf16[256,3,128]{2,0,1:T(8,128)(2,1)}), bf16[2048,3,128]{2,0,1:T(8,128)(2,1)}) %all-gather.17.cloned.1.call-update) | async-done | bytes 1572880 | tf_op jit(solution)/shard_map/all_gather | solution.py:205
  252.1 61.9 %all-gather.23.cloned.1.call-done = bf16[2359296]{0:T(1024)(128)(2,1)} async-done(((bf16[73728]{0:T(1024)(128)(2,1)}), bf16[2359296]{0:T(1024)(128)(2,1)}) %all-gather.23.cloned.1.call-update) | async-done | bytes 4718608 | tf_op jit(solution)/shard_map/all_gather | solution.py:64
  314.0 8.2 reshape.889
  322.2 57.2 %all-gather.25.cloned.1.call-done = bf16[2359296]{0:T(1024)(128)(2,1)} async-done(((bf16[73728]{0:T(1024)(128)(2,1)}), bf16[2359296]{0:T(1024)(128)(2,1)}) %all-gather.25.cloned.1.call-update) | async-done | bytes 4718608 | tf_op jit(solution)/shard_map/all_gather | solution.py:65
  379.4 9.2 reshape.890
  394.3 24.6 %while.79 = (s32[]{:T(128)}, f32[3,256]{1,0:T(4,128)S(1)}, f32[3,256]{1,0:T(4,128)S(1)}, f32[256,3,64]{0,2,1:T(8,128)S(1)}, s32[256]{0:T(256)S(1)}, /*index=5*/s...) while((s32[]{:T(128)}, f32[3,256]{1,0:T(4,128)S(1)}, ...), condition=%wide.region_15.16_spmd.clone, body=%wide.region_12.15_spmd.clone.sunk | while | flops 77583360 | bytes 4218509 | solution.py:200
  420.0 5.0 all-to-all-start.5
  426.6 10.0 all_gather.90
  436.7 30.1 %while.78 = (s32[]{:T(128)}, f32[3,256]{1,0:T(4,128)S(1)}, f32[3,256]{1,0:T(4,128)S(1)}, f32[256,3,64]{0,2,1:T(8,128)S(1)}, s32[256]{0:T(256)S(1)}, /*index=5*/s...) while((s32[]{:T(128)}, f32[3,256]{1,0:T(4,128)S(1)}, ...), condition=%wide.region_5.6_spmd.clone, body=%wide.region_2.5_spmd.clone.sunk | while | flops 77583360 | bytes 4218509 | solution.py:200
  467.9 9.0 all_gather.86
  476.9 5.5 all-to-all-start.2
  515.0 5.1 fusion.241
  520.1 5.3 fusion.249
  533.4 9.3 convolution_add_fusion
  542.7 5.1 add_bitcast_fusion
  555.4 10.7 reshape.915
  566.1 9.6 copy.467
  575.7 5.0 all-to-all-start.9
  582.2 23.1 %while.80 = (s32[]{:T(128)}, f32[256,3,128]{0,2,1:T(8,128)S(1)}, bf16[8,256,3,128]{3,1,2,0:T(8,128)(2,1)}, s32[8,256]{1,0:T(8,128)}, s32[256]{0:T(256)S(1)}, /*i...) while((s32[]{:T(128)}, f32[256,3,128]{0,2,1:T(8,128)S(1)}, ...), condition=%wide.region_26.27_spmd.clone, body=%wide.region_25.26_spmd.clone.sunk | while | flops 128254464 | bytes 4077203 | solution.py:296
  606.4 5.1 all-to-all-start.7
  613.0 23.0 %while.82 = (s32[]{:T(128)}, f32[256,3,128]{0,2,1:T(8,128)S(1)}, bf16[8,256,3,128]{3,1,2,0:T(8,128)(2,1)}, s32[8,256]{1,0:T(8,128)S(1)}, s32[256]{0:T(256)S(1)},...) while((s32[]{:T(128)}, f32[256,3,128]{0,2,1:T(8,128)S(1)}, ...), condition=%wide.region_35.36_spmd.clone, body=%wide.region_34.35_spmd.clone.sunk | while | flops 128254464 | bytes 4077203 | solution.py:296
  637.7 5.3 all-to-all-start.10
  643.0 12.1 all_gather.91
  656.2 13.5 all_gather.87
  669.8 8.0 all_gather.88
  677.8 9.1 all_gather.92
  690.4 5.1 add_bitcast_fusion.1
  695.5 12.1 copy.443
  707.6 12.4 reshape.911
  720.0 38.3 %while.83 = (s32[]{:T(128)}, f32[256,3,128]{0,2,1:T(8,128)S(1)}, f32[256,3,64]{0,2,1:T(8,128)S(1)}, bf16[8,256,3,128]{3,1,0,2:T(8,128)(2,1)}, s32[256]{0:T(256)S...) while((s32[]{:T(128)}, f32[256,3,128]{0,2,1:T(8,128)S(1)}, ...), condition=%wide.region_37.38_spmd.clone, body=%wide.region_36.37_spmd.clone.sunk | while | flops 152829952 | bytes 4578975 | solution.py:359
  764.2 31.3 %while.81 = (s32[]{:T(128)}, f32[256,3,128]{0,2,1:T(8,128)S(1)}, f32[256,3,64]{0,2,1:T(8,128)S(1)}, bf16[8,256,3,128]{3,1,0,2:T(8,128)(2,1)}, s32[256]{0:T(256)S...) while((s32[]{:T(128)}, f32[256,3,128]{0,2,1:T(8,128)S(1)}, ...), condition=%wide.region_28.29_spmd.clone, body=%wide.region_27.28_spmd.clone.sunk | while | flops 152829952 | bytes 4579999 | solution.py:359
  796.5 5.1 all-to-all-start.8
  802.7 7.7 all-to-all-done.8
  815.1 8.2 copy.444
  823.4 7.3 reshape.912
  840.9 5.0 fusion.166
  846.3 42.5 %all-reduce.5 = (f32[4,768]{1,0:T(4,128)}, f32[768]{0:T(1024)}, f32[768]{0:T(1024)}, f32[768]{0:T(1024)}, f32[768]{0:T(1024)}, /*index=5*/f32[3072]{0:T(1024)}, f32[768]{0:T(1024)}, f32[768]{0:T(1024)}, f32[768]{0:T(1024)}) all-reduce(f32[4,768]{1,0:T(4,128)S(1)} %copy-done.56, ...), channel_id=1, replica_groups=mesh['head'=4,'blk'=8] {'head','blk'}, use_global_device_ids=true, to_apply=%region_41.42 | all-reduce | flops 11520 | bytes 92160 | tf_op jit(solution)/shard_map/psum | solution.py:413
  893.0 466.2 %all-reduce.9.cloned.1.call-done = (f32[2359296]{0:T(1024)}, f32[1179648]{0:T(1024)}, f32[589824]{0:T(1024)}, f32[2359296]{0:T(1024)}, f32[2359296]{0:T(1024)}) async-done(((f32[2359296]{0:T(1024)}, f32[1179648]{0:T(1024)}, f32[589824]{0:T(1024)}, f32[2359296]{0:T(1024)}, f32[2359296]{0:T(1024)}), (f32[2359296]{0:T(1024)}, f32[1179648]{0:T(1024)}, f32[589824]{0:T(1024)}, f32[2359296]{0:T(1024)}, ...) | async-done | bytes 35389456
  (919 shorter events, 336.0 us)
Async XLA Ops:
  7.2 68.5 %copy-start.16 = (bf16[2,64,768]{2,1,0:T(8,128)(2,1)S(1)}, bf16[2,64,768]{2,1,0:T(8,128)(2,1)}, u32[]{:S(2)}) copy-start(bf16[2,64,768]{2,1,0:T(8,128)(2,1)} %param.30) | copy-start | bytes 589828
  7.2 63.7 %all-gather.15.cloned.1.call-start = ((), (), s32[]{:S(2)}) async-start(), calls=%async_computation.12 | async-start | bytes 2433024 | tf_op jit(solution)/shard_map/all_gather | solution.py:57
  7.9 151.2 %all-gather.21.cloned.1.call-start = ((), (), s32[]{:S(2)}) async-start(), calls=%async_computation.15 | async-start | bytes 1216512 | tf_op jit(solution)/shard_map/all_gather | solution.py:58
  8.7 184.5 %all-gather.19.cloned.1.call-start = ((), (), s32[]{:S(2)}) async-start(), calls=%async_computation.14 | async-start | bytes 4866048 | tf_op jit(solution)/shard_map/all_gather | solution.py:56
  9.4 220.8 %all-gather.27.cloned.1.call-start = ((), (), s32[]{:S(2)}) async-start(), calls=%async_computation.18 | async-start | bytes 1769472 | tf_op jit(solution)/shard_map/all_gather | solution.py:205
  77.8 30.8 %copy-start.98 = (bf16[768]{0:T(1024)(128)(2,1)S(1)}, bf16[768]{0:T(1024)(128)(2,1)}, u32[]{:S(2)}) copy-start(bf16[768]{0:T(1024)(128)(2,1)} %param.40) | copy-start | bytes 4612
  77.8 30.8 %copy-start.99 = (bf16[768]{0:T(1024)(128)(2,1)S(1)}, bf16[768]{0:T(1024)(128)(2,1)}, u32[]{:S(2)}) copy-start(bf16[768]{0:T(1024)(128)(2,1)} %param.41) | copy-start | bytes 4612
  77.8 30.8 %copy-start.100 = (bf16[768]{0:T(1024)(128)(2,1)S(1)}, bf16[768]{0:T(1024)(128)(2,1)}, u32[]{:S(2)}) copy-start(bf16[768]{0:T(1024)(128)(2,1)} %param.39) | copy-start | bytes 4612
  77.8 31.4 %copy-start.101 = (bf16[768]{0:T(1024)(128)(2,1)S(1)}, bf16[768]{0:T(1024)(128)(2,1)}, u32[]{:S(2)}) copy-start(bf16[768]{0:T(1024)(128)(2,1)} %param.45) | copy-start | bytes 4612
  77.8 32.0 %copy-start.102 = (bf16[768]{0:T(1024)(128)(2,1)S(1)}, bf16[768]{0:T(1024)(128)(2,1)}, u32[]{:S(2)}) copy-start(bf16[768]{0:T(1024)(128)(2,1)} %param.46) | copy-start | bytes 4612
  77.9 32.6 %copy-start.103 = (bf16[768]{0:T(1024)(128)(2,1)S(1)}, bf16[768]{0:T(1024)(128)(2,1)}, u32[]{:S(2)}) copy-start(bf16[768]{0:T(1024)(128)(2,1)} %param.47) | copy-start | bytes 4612
  77.9 33.2 %copy-start.73 = (s32[2,64]{1,0:T(2,128)S(1)}, s32[2,64]{1,0:T(2,128)}, u32[]{:S(2)}) copy-start(s32[2,64]{1,0:T(2,128)} %param.31) | copy-start | bytes 1540
  77.9 61.5 %copy-start.90 = (bf16[4,768]{1,0:T(4,128)(2,1)S(1)}, bf16[4,768]{1,0:T(4,128)(2,1)}, u32[]{:S(2)}) copy-start(bf16[4,768]{1,0:T(4,128)(2,1)} %param.35) | copy-start | bytes 18436
  77.9 61.5 %copy-start.91 = (bf16[3072]{0:T(1024)(128)(2,1)S(1)}, bf16[3072]{0:T(1024)(128)(2,1)}, u32[]{:S(2)}) copy-start(bf16[3072]{0:T(1024)(128)(2,1)} %param.43) | copy-start | bytes 18436
  77.9 61.5 %copy-start.104 = (s32[2,32]{1,0:T(2,128)S(1)}, s32[2,32]{1,0:T(2,128)}, u32[]{:S(2)}) copy-start(s32[2,32]{1,0:T(2,128)} %param.32) | copy-start | bytes 772
  94.2 69.6 %copy-start.19 = (bf16[4,64,3,128]{3,1,0,2:T(8,128)(2,1)S(1)}, bf16[4,64,3,128]{3,1,0,2:T(8,128)(2,1)}, u32[]{:S(2)}) copy-start(bf16[4,64,3,128]{3,1,0,2:T(8,128)(2,1)} %copy.398) | copy-start | bytes 589828
  94.2 153.4 %all-gather.17.cloned.1.call-start = ((), (), s32[]{:S(2)}) async-start(), calls=%async_computation.13 | async-start | bytes 1769472 | tf_op jit(solution)/shard_map/all_gather | solution.py:205
  107.2 206.8 %all-gather.23.cloned.1.call-start = ((), (), s32[]{:S(2)}) async-start(), calls=%async_computation.16 | async-start | bytes 4866048 | tf_op jit(solution)/shard_map/all_gather | solution.py:64
  107.8 271.6 %all-gather.25.cloned.1.call-start = ((), (), s32[]{:S(2)}) async-start(), calls=%async_computation.17 | async-start | bytes 4866048 | tf_op jit(solution)/shard_map/all_gather | solution.py:65
  119.9 82.6 %copy-start.86 = (f32[1,256]{1,0:T(1,128)}, f32[1,256]{1,0:T(1,128)S(1)}, u32[]{:S(2)}) copy-start(f32[1,256]{1,0:T(1,128)S(1)} %get-tuple-element.1129) | copy-start | bytes 3076
  119.9 82.6 %copy-start.88 = (f32[1,256]{1,0:T(1,128)}, f32[1,256]{1,0:T(1,128)S(1)}, u32[]{:S(2)}) copy-start(f32[1,256]{1,0:T(1,128)S(1)} %get-tuple-element.1130) | copy-start | bytes 3076
  164.7 37.8 %copy-start.17 = (bf16[2,64,768]{2,1,0:T(8,128)(2,1)S(1)}, bf16[2,64,768]{2,1,0:T(8,128)(2,1)}, u32[]{:S(2)}) copy-start(bf16[2,64,768]{2,1,0:T(8,128)(2,1)} %param.30) | copy-start | bytes 589828
  219.6 169.0 %all-to-all-start.4 = ((bf16[64,12,128]{2,0,1:T(8,128)(2,1)}), bf16[64,12,128]{2,0,1:T(8,128)(2,1)}, u32[]{:S(2)}, u32[]{:S(2)}) async-start(bf16[64,12,128]{2,0,1:T(8,128)(2,1)} %copy.400), calls=%async_computation.4 | async-start | bytes 393216 | tf_op jit(solution)/shard_map/all_to_all | solution.py:158
  388.6 31.4 %all-to-all-start.1 = ((bf16[64,12,128]{2,0,1:T(8,128)(2,1)}), bf16[64,12,128]{2,0,1:T(8,128)(2,1)}, u32[]{:S(2)}, u32[]{:S(2)}) async-start(bf16[64,12,128]{2,0,1:T(8,128)(2,1)} %copy.390), calls=%async_computation.1 | async-start | bytes 393216 | tf_op jit(solution)/shard_map/all_to_all | solution.py:158
  392.6 327.3 %all-gather.31.cloned.1.call-start = ((), (), s32[]{:S(2)}) async-start(), calls=%async_computation.20 | async-start | bytes 1769472 | tf_op jit(solution)/shard_map/all_gather | solution.py:351
  420.0 57.0 %all-to-all-start.5 = ((bf16[4,2,6144]{2,1,0:T(2,128)(2,1)}), bf16[4,2,6144]{2,1,0:T(2,128)(2,1)S(1)}, u32[]{:S(2)}, u32[]{:S(2)}) async-start(bf16[4,2,6144]{2,1,0:T(2,128)(2,1)} %reshape.963), calls=%async_computation.5 | async-start | bytes 196608 | tf_op jit(solution)/shard_map/all_to_all | solution.py:214
  425.0 339.2 %all-gather.29.cloned.1.call-start = ((), (), s32[]{:S(2)}) async-start(), calls=%async_computation.19 | async-start | bytes 1769472 | tf_op jit(solution)/shard_map/all_gather | solution.py:351
  436.6 46.3 %copy-start.58 = (f32[768]{0:T(1024)S(1)}, f32[768]{0:T(1024)}, u32[]{:S(2)}) copy-start(f32[768]{0:T(1024)} %convert_element_type.299) | copy-start | bytes 9220
  476.9 11.2 all-to-all-start.2
  529.3 46.3 %all-to-all-start.6 = ((bf16[4,2,6144]{2,1,0:T(2,128)(2,1)}), bf16[4,2,6144]{2,1,0:T(2,128)(2,1)}, u32[]{:S(2)}, u32[]{:S(2)}) async-start(bf16[4,2,6144]{2,1,0:T(2,128)(2,1)} %reshape.969), calls=%async_computation.6 | async-start | bytes 196608 | tf_op jit(solution)/shard_map/all_to_all | solution.py:262
  575.7 30.8 %all-to-all-start.9 = ((bf16[4,2,6144]{2,1,0:T(2,128)(2,1)}), bf16[4,2,6144]{2,1,0:T(2,128)(2,1)}, u32[]{:S(2)}, u32[]{:S(2)}) async-start(bf16[4,2,6144]{2,1,0:T(2,128)(2,1)} %reshape.967), calls=%async_computation.9 | async-start | bytes 196608 | tf_op jit(solution)/shard_map/all_to_all | solution.py:262
  582.2 30.8 %copy-start.9 = (bf16[256,3,128]{2,0,1:T(8,128)(2,1)S(1)}, bf16[256,3,128]{2,0,1:T(8,128)(2,1)}, u32[]{:S(2)}) copy-start(bf16[256,3,128]{2,0,1:T(8,128)(2,1)} %get-tuple-element.1815) | copy-start | bytes 589828
  606.4 30.6 %all-to-all-start.7 = ((bf16[256,3,128]{2,1,0:T(4,128)(2,1)}), bf16[256,3,128]{2,1,0:T(4,128)(2,1)S(1)}, u32[]{:S(2)}, u32[]{:S(2)}) async-start(bf16[256,3,128]{2,1,0:T(4,128)(2,1)} %copy.409), calls=%async_computation.7 | async-start | bytes 524288 | tf_op jit(solution)/shard_map/all_to_all | solution.py:364
  637.7 49.3 %all-to-all-start.10 = ((bf16[256,3,128]{2,1,0:T(4,128)(2,1)}), bf16[256,3,128]{2,1,0:T(4,128)(2,1)S(1)}, u32[]{:S(2)}, u32[]{:S(2)}) async-start(bf16[256,3,128]{2,1,0:T(4,128)(2,1)} %copy.428), calls=%async_computation.10 | async-start | bytes 524288 | tf_op jit(solution)/shard_map/all_to_all | solution.py:364
  643.0 43.9 %copy-start.30 = (bf16[256,3,128]{2,1,0:T(4,128)(2,1)S(1)}, bf16[256,3,128]{2,1,0:T(4,128)(2,1)}, u32[]{:S(2)}) copy-start(bf16[256,3,128]{2,1,0:T(4,128)(2,1)} %copy-done.29) | copy-start | bytes 589828
  656.2 32.4 %copy-start.96 = (bf16[64]{0:T(256)(128)(2,1)S(1)}, bf16[64]{0:T(256)(128)(2,1)}, u32[]{:S(2)}) copy-start(bf16[64]{0:T(256)(128)(2,1)} %get-tuple-element.1137) | copy-start | bytes 388
  656.2 32.4 %copy-start.97 = (bf16[64]{0:T(256)(128)(2,1)S(1)}, bf16[64]{0:T(256)(128)(2,1)}, u32[]{:S(2)}) copy-start(bf16[64]{0:T(256)(128)(2,1)} %get-tuple-element.1139) | copy-start | bytes 388
  656.2 32.6 %copy-start.94 = (bf16[64]{0:T(256)(128)(2,1)S(1)}, bf16[64]{0:T(256)(128)(2,1)}, u32[]{:S(2)}) copy-start(bf16[64]{0:T(256)(128)(2,1)} %get-tuple-element.1138) | copy-start | bytes 388
  656.2 32.6 %copy-start.95 = (bf16[64]{0:T(256)(128)(2,1)S(1)}, bf16[64]{0:T(256)(128)(2,1)}, u32[]{:S(2)}) copy-start(bf16[64]{0:T(256)(128)(2,1)} %get-tuple-element.1140) | copy-start | bytes 388
  720.0 38.3 %copy-start.89 = (f32[1,256]{1,0:T(1,128)S(1)}, f32[1,256]{1,0:T(1,128)}, u32[]{:S(2)}) copy-start(f32[1,256]{1,0:T(1,128)} %copy-done.88) | copy-start | bytes 3076
  720.0 38.3 %copy-start.93 = (f32[256]{0:T(256)S(1)}, f32[256]{0:T(256)}, u32[]{:S(2)}) copy-start(f32[256]{0:T(256)} %broadcast_subtract_fusion.4) | copy-start | bytes 3076
  720.0 44.1 %copy-start.13 = (f32[256,3,64]{0,2,1:T(8,128)S(1)}, f32[256,3,64]{0,2,1:T(8,128)}, u32[]{:S(2)}) copy-start(f32[256,3,64]{0,2,1:T(8,128)} %custom-call.8) | copy-start | bytes 589828
  759.3 37.2 %all-to-all-start.11 = ((bf16[256,3,128]{2,1,0:T(4,128)(2,1)}), bf16[256,3,128]{2,1,0:T(4,128)(2,1)S(1)}, u32[]{:S(2)}, u32[]{:S(2)}) async-start(bf16[256,3,128]{2,1,0:T(4,128)(2,1)} %copy.437), calls=%async_computation.11 | async-start | bytes 524288 | tf_op jit(solution)/shard_map/all_to_all | solution.py:367
  764.1 31.4 %copy-start.87 = (f32[1,256]{1,0:T(1,128)S(1)}, f32[1,256]{1,0:T(1,128)}, u32[]{:S(2)}) copy-start(f32[1,256]{1,0:T(1,128)} %copy-done.86) | copy-start | bytes 3076
  764.1 31.4 %copy-start.92 = (f32[256]{0:T(256)S(1)}, f32[256]{0:T(256)}, u32[]{:S(2)}) copy-start(f32[256]{0:T(256)} %broadcast_subtract_fusion.5) | copy-start | bytes 3076
  796.5 13.9 %all-to-all-start.8 = ((bf16[256,3,128]{2,1,0:T(4,128)(2,1)}), bf16[256,3,128]{2,1,0:T(4,128)(2,1)S(1)}, u32[]{:S(2)}, u32[]{:S(2)}) async-start(bf16[256,3,128]{2,1,0:T(4,128)(2,1)} %copy.418), calls=%async_computation.8 | async-start | bytes 524288 | tf_op jit(solution)/shard_map/all_to_all | solution.py:367
  801.6 557.7 %all-reduce.9.cloned.1.call-start = ((), (), s32[]{:S(2)}) async-start(), calls=%async_computation.21 | async-start | bytes 70778880
  840.8 47.9 %copy-start.1 = (bf16[768,2,768]{2,1,0:T(2,128)(2,1)S(1)}, bf16[768,2,768]{2,1,0:T(2,128)(2,1)}, u32[]{:S(2)}) copy-start(bf16[768,2,768]{2,1,0:T(2,128)(2,1)} %copy-done) | copy-start | bytes 7077892
  (86 other events, 593.6 us)
Sparse Core Ops, SparseCore 0:
  10.9 59.9 all-gather.14
  73.8 53.7 all-gather.20
  130.5 62.6 all-gather.18
  195.0 24.4 all-gather.26
  221.8 25.6 all-gather.16
  250.3 63.6 all-gather.22
  316.9 62.4 all-gather.24
  395.9 26.1 all-gather.30
  436.8 26.1 all-gather.28
  831.0 528.2 all-reduce.8
where the time goes:
time: 1390 us; the launch traced here: 1370 us
  waiting for transfers between devices  704 us (51%)
  local copies, waits for them, and re-layouts  194 us (14%)
  matrix products  183 us (13%)
  blocking collectives  169 us (12%)
  other arithmetic  56.6 us (4%)
  starting transfers between devices  48.5 us (3%)
  between operations  16.8 us (1%)
    unnamed x11, waiting for transfers between devices  470 us
    all_gather x1, waiting for transfers between devices, fetch_feedforward(): lax.all_gather(inner_weight, ('head', 'blk'), axis=0, tiled=True)  61.9 us
    all_gather x1, waiting for transfers between devices, fetch_attention(): lax.all_gather(keyval_weight, ('head', 'blk'), axis=0, tiled=True)  60.7 us
    all_gather x1, waiting for transfers between devices, fetch_feedforward(): lax.all_gather(outer_weight, ('head', 'blk'), axis=0, tiled=True)  57.2 us
    psum x1, blocking collectives, body(): lax.psum((sum_qoffset, sum_voffset, sum_ooffset, sum_gain_first, sum_shif...  42.5 us
    unnamed x251, local copies, waits for them, and re-layouts  35.7 us
    squeeze x32, local copies, waits for them, and re-layouts, body(): lax.scan(attend_advance, start_state, split_rows((lax.all_gather(keyval_h...  30.3 us
    all_gather x1, waiting for transfers between devices, fetch_attention(): lax.all_gather(query_weight, ('head', 'blk'), axis=0, tiled=True)  28.5 us
  transfers between devices with their start and end apart: 20, of which 8 were waited for; matrix products, arithmetic and copies ran while one was open for 29% of the time, Pallas kernels for 0%

commit v1 on v0

v1 whole, which is shorter than its diff:
```python
import math

import jax
import jax.numpy as jnp
from jax import lax
from jax.experimental import pallas as pl
from jax.experimental.pallas import tpu as pltpu
from jax.sharding import PartitionSpec as P

HEADS = 12
HD = 64
WIDE = 2 * HD
EPS = 1e-12
GELU_A = math.sqrt(2.0 / math.pi)
GELU_B = 0.044715
F32 = jnp.float32
BF16 = jnp.bfloat16
NEG = -1e30
VMEM_BYTES = 58 * 1024 * 1024


def any_spec():
    return pl.BlockSpec(memory_space=pl.ANY)


def vmem_spec():
    return pl.BlockSpec(memory_space=pltpu.VMEM)


def smem_spec():
    return pl.BlockSpec(memory_space=pltpu.SMEM)


def dot(a, b):
    return lax.dot_general(a, b, (((1,), (0,)), ((), ())), preferred_element_type=F32)


def dot_tn(a, b):
    return lax.dot_general(a, b, (((0,), (0,)), ((), ())), preferred_element_type=F32)


def dot_nt(a, b):
    return lax.dot_general(a, b, (((1,), (1,)), ((), ())), preferred_element_type=F32)


def project_kernel(groups, heads, w_col, place, x_refs, w_hbm, bias, flag, q_out, kv_out, x_out, w, sem):
    rows = x_refs[0].shape[0]
    cols = w.shape[1]
    half = heads * WIDE
    copy = pltpu.make_async_copy(
        w_hbm.at[:, pl.ds(pl.multiple_of(w_col + place[0] * cols, 128), cols)], w, sem
    )
    copy.start()
    copy.wait()
    for step in range(groups):
        seg = lax.rem(place[0] + (groups - step), groups)
        x = x_refs[step][...]
        x_out[seg] = x
        y = dot(x, w[...]) + bias[...]
        entity = flag[seg] == 1.0
        for h in range(heads):
            word = y[:, h * WIDE : (h + 1) * WIDE]
            ent = y[:, half + h * WIDE : half + (h + 1) * WIDE]
            q_out[h, seg] = jnp.where(entity, ent, word).astype(BF16)
            kv_out[h, seg] = y[:, 2 * half + h * WIDE : 2 * half + (h + 1) * WIDE].astype(BF16)


def project(place, xs, w, bias, flag, heads):
    groups = len(xs)
    rows, width = xs[0].shape
    cols = bias.shape[1]

    def kernel(place_ref, *refs):
        x_refs = refs[:groups]
        project_kernel(groups, heads, 0, place_ref, x_refs, *refs[groups:])

    return pl.pallas_call(
        kernel,
        out_shape=(
            jax.ShapeDtypeStruct((heads, groups, rows, WIDE), BF16),
            jax.ShapeDtypeStruct((heads, groups, rows, WIDE), BF16),
            jax.ShapeDtypeStruct((groups, rows, width), BF16),
        ),
        in_specs=[smem_spec()] + [vmem_spec()] * groups + [any_spec(), vmem_spec(), vmem_spec()],
        out_specs=(vmem_spec(), vmem_spec(), vmem_spec()),
        scratch_shapes=[pltpu.VMEM((width, cols), BF16), pltpu.SemaphoreType.DMA],
        compiler_params=pltpu.CompilerParams(vmem_limit_bytes=VMEM_BYTES),
        cost_estimate=pl.CostEstimate(
            flops=2 * groups * rows * width * cols, bytes_accessed=4 * width * cols, transcendentals=0
        ),
        name="project",
    )(place, *xs, w, bias, flag)


def flag_of(code):
    code = code.astype(F32)
    return code - 2.0 * jnp.floor(0.5 * code)


def chunk_of(length):
    return min(512, length)


def attend_kernel(
    groups, heads, blocks, place, span, q, *refs
):
    kv_pieces = refs[:blocks]
    code_k, doc_q = refs[blocks : blocks + 2]
    ctx_out, lse_out, kv_out, wk_out = refs[blocks + 2 : blocks + 6]
    kv_sem = refs[blocks + 6]
    rows = q.shape[2]
    length = groups * blocks * rows
    chunk = chunk_of(length)
    scale = 1.0 / math.sqrt(HD)
    copies = []
    for p in range(blocks):
        at = place[1] ^ p
        for h in range(heads):
            for g in range(groups):
                start = pl.multiple_of((g * blocks + at) * rows, rows)
                copies.append(
                    pltpu.make_async_copy(
                        kv_pieces[p].at[h, g], kv_out.at[h, pl.ds(start, rows)], kv_sem
                    )
                )
    for c in copies:
        c.start()
    for c in copies:
        c.wait()
    lane = lax.broadcasted_iota(jnp.int32, (1, WIDE), 1) < HD

    def widen(i, _):
        at = pl.ds(pl.multiple_of(i * chunk, chunk), chunk)
        flag = flag_of(code_k[at, :])
        share = jnp.where(lane, 1.0 - flag, flag)
        for h in range(heads):
            kv = kv_out[h, at, :].astype(F32)
            both = jnp.where(lane, kv, pltpu.roll(kv, HD, 1))
            wk_out[h, at, :] = (both * share).astype(BF16)
        return 0

    lax.fori_loop(0, length // chunk, widen, 0)

    for seg in range(groups):
        dq = 2.0 * doc_q[seg : seg + 1, :] + 0.5
        qt = [q[h, seg].T for h in range(heads)]

        def step(i, carry):
            at = pl.ds(pl.multiple_of(i * chunk, chunk), chunk)
            same = jnp.abs(code_k[at, :].astype(F32) - dq) < 1.0
            out = []
            for h in range(heads):
                m, l, acc = carry[h]
                s = dot(wk_out[h, at, :], qt[h]) * scale
                s = jnp.where(same, s, NEG)
                m_new = jnp.maximum(m, jnp.max(s, 0, keepdims=True))
                factor = jnp.exp(m - m_new)
                p = jnp.exp(s - m_new)
                l = l * factor + jnp.sum(p, 0, keepdims=True)
                acc = acc * factor + dot_tn(kv_out[h, at, :], p.astype(BF16))
                out.append((m_new, l, acc))
            return tuple(out)

        start = tuple(
            (jnp.full((1, rows), NEG, F32), jnp.zeros((1, rows), F32), jnp.zeros((WIDE, rows), F32))
            for _ in range(heads)
        )
        done = lax.fori_loop(span[seg, 0], span[seg, 1], step, start)
        parts = []
        for h in range(heads):
            m, l, acc = done[h]
            lse_out[seg * heads + h : seg * heads + h + 1, :] = m + jnp.log(l)
            parts.append(acc[HD:, :] / l)
        ctx_out[seg] = jnp.concatenate(parts, 0).T.astype(BF16)


def attend(place, span, q, pieces, code_k, doc_q):
    heads, groups, rows, _ = q.shape
    blocks = len(pieces)
    length = groups * blocks * rows
    flops = 4 * heads * groups * rows * length * WIDE // 2

    def kernel(place_ref, span_ref, q_ref, *refs):
        attend_kernel(groups, heads, blocks, place_ref, span_ref, q_ref, *refs)

    return pl.pallas_call(
        kernel,
        out_shape=(
            jax.ShapeDtypeStruct((groups, rows, heads * HD), BF16),
            jax.ShapeDtypeStruct((groups * heads, rows), F32),
            jax.ShapeDtypeStruct((heads, length, WIDE), BF16),
            jax.ShapeDtypeStruct((heads, length, WIDE), BF16),
        ),
        in_specs=[smem_spec(), smem_spec(), vmem_spec()]
        + [any_spec()] * blocks
        + [vmem_spec()] * 2,
        out_specs=(vmem_spec(), vmem_spec(), vmem_spec(), vmem_spec()),
        scratch_shapes=[pltpu.SemaphoreType.DMA],
        compiler_params=pltpu.CompilerParams(vmem_limit_bytes=VMEM_BYTES),
        cost_estimate=pl.CostEstimate(
            flops=flops, bytes_accessed=4 * heads * length * WIDE, transcendentals=0
        ),
        name="attend",
    )(place, span, q, *pieces, code_k, doc_q)


def attend_back_kernel(
    groups, heads, blocks, place, span, q, kv, wk, ctx, lse, code_k, doc_q, *refs
):
    dctx = refs[:groups]
    dq_out, dkv_out, acc, stage, sem = refs[groups:]
    rows = q.shape[2]
    length = kv.shape[1]
    chunk = chunk_of(length)
    scale = 1.0 / math.sqrt(HD)
    lane = lax.broadcasted_iota(jnp.int32, (1, WIDE), 1) < HD

    def clear(i, _):
        at = pl.ds(pl.multiple_of(i * chunk, chunk), chunk)
        for h in range(heads):
            acc[h, at, :] = jnp.zeros((chunk, WIDE), F32)
        return 0

    lax.fori_loop(0, length // chunk, clear, 0)

    for step_of in range(groups):
        seg = lax.rem(place[0] + (groups - step_of), groups)
        d_t = dctx[step_of][...].astype(F32).T
        c_t = ctx[seg].astype(F32).T
        prod = d_t * c_t
        dq_row = 2.0 * doc_q[pl.ds(seg, 1), :] + 0.5
        qs, qt, d_pad_t, d_pad, deltas, lses = [], [], [], [], [], []
        for h in range(heads):
            qh = q[h, seg]
            qs.append(qh)
            qt.append(qh.T)
            padded = jnp.concatenate(
                [jnp.zeros((HD, rows), F32), d_t[h * HD : (h + 1) * HD, :]], 0
            )
            d_pad_t.append(padded.astype(BF16))
            d_pad.append(padded.T.astype(BF16))
            deltas.append(jnp.sum(prod[h * HD : (h + 1) * HD, :], 0, keepdims=True))
            lses.append(lse[pl.ds(seg * heads + h, 1), :])

        def step(i, carry):
            at = pl.ds(pl.multiple_of(i * chunk, chunk), chunk)
            code = code_k[at, :].astype(F32)
            same = jnp.abs(code - dq_row) < 1.0
            flag = flag_of(code)
            share = jnp.where(lane, 1.0 - flag, flag) * scale
            out = []
            for h in range(heads):
                wide = wk[h, at, :]
                s = dot(wide, qt[h]) * scale
                p = jnp.exp(jnp.where(same, s, NEG) - lses[h])
                dp = dot(kv[h, at, :], d_pad_t[h])
                ds = (p * (dp - deltas[h])).astype(BF16)
                dv = dot(p.astype(BF16), d_pad[h])
                dw = dot(ds, qs[h]) * share
                acc[h, at, :] += jnp.where(lane, dw + pltpu.roll(dw, HD, 1), dv)
                out.append(carry[h] + dot_tn(wide, ds))
            return tuple(out)

        done = lax.fori_loop(
            span[seg, 0],
            span[seg, 1],
            step,
            tuple(jnp.zeros((WIDE, rows), F32) for _ in range(heads)),
        )
        for h in range(heads):
            dq_out[h, seg] = (done[h].T * scale).astype(BF16)

    def out_copy(p):
        return pltpu.make_async_copy(stage.at[p % 2], dkv_out.at[p], sem.at[p % 2])

    for p in range(blocks):
        at = place[1] ^ p
        if p >= 2:
            out_copy(p - 2).wait()
        for h in range(heads):
            for g in range(groups):
                start = pl.multiple_of((g * blocks + at) * rows, rows)
                stage[p % 2, h, g] = acc[h, pl.ds(start, rows), :].astype(BF16)
        out_copy(p).start()
    for p in range(max(0, blocks - 2), blocks):
        out_copy(p).wait()


def attend_back(place, span, q, kv, wk, ctx, lse, code_k, doc_q, dctx):
    heads, groups, rows, _ = q.shape
    length = kv.shape[1]
    blocks = length // (groups * rows)

    def kernel(place_ref, span_ref, *refs):
        attend_back_kernel(groups, heads, blocks, place_ref, span_ref, *refs)

    return pl.pallas_call(
        kernel,
        out_shape=(
            jax.ShapeDtypeStruct((heads, groups, rows, WIDE), BF16),
            jax.ShapeDtypeStruct((blocks, heads, groups, rows, WIDE), BF16),
        ),
        in_specs=[smem_spec(), smem_spec()] + [vmem_spec()] * (7 + groups),
        out_specs=(vmem_spec(), any_spec()),
        scratch_shapes=[
            pltpu.VMEM((heads, length, WIDE), F32),
            pltpu.VMEM((2, heads, groups, rows, WIDE), BF16),
            pltpu.SemaphoreType.DMA((2,)),
        ],
        compiler_params=pltpu.CompilerParams(vmem_limit_bytes=VMEM_BYTES),
        cost_estimate=pl.CostEstimate(
            flops=10 * heads * groups * rows * length * WIDE // 2,
            bytes_accessed=8 * heads * length * WIDE,
            transcendentals=0,
        ),
        name="attend_back",
    )(place, span, q, kv, wk, ctx, lse, code_k, doc_q, *dctx)


def norm(v, gain, shift):
    centred = v - jnp.mean(v, -1, keepdims=True)
    inverse = lax.rsqrt(jnp.mean(centred * centred, -1, keepdims=True) + EPS)
    normed = centred * inverse
    return normed * gain + shift, normed, inverse


def norm_back(g, normed, inverse, gain):
    scaled = g * gain
    inward = inverse * (
        scaled
        - jnp.mean(scaled, -1, keepdims=True)
        - normed * jnp.mean(scaled * normed, -1, keepdims=True)
    )
    return inward, jnp.sum(g * normed, 0, keepdims=True), jnp.sum(g, 0, keepdims=True)


def middle_kernel(
    groups, parts, w_col, place, x, cot, vec, w_hbm, *refs
):
    ctx = refs[:groups]
    out, g_hbm, dsum_out, vec_out = refs[groups : groups + 4]
    dctx = refs[groups + 4 : 2 * groups + 4]
    w, g, inner_s, act_s, w_sem, g_sem = refs[2 * groups + 4 :]
    width = x.shape[1]
    share = width // groups

    def w_copy(j):
        return pltpu.make_async_copy(
            w_hbm.at[:, pl.ds(w_col + j * width, width)], w.at[j], w_sem.at[j]
        )

    def g_copy(j):
        return pltpu.make_async_copy(
            g.at[j], g_hbm.at[:, pl.ds(j * width, width)], g_sem.at[j]
        )

    blocks = 1 + 2 * parts
    order = [0] + [i for j in range(parts) for i in (1 + j, 1 + parts + j)]
    for j in order:
        w_copy(j).start()
    srcs = [lax.rem(place[0] + (groups - d), groups) for d in range(groups)]

    def rows_of(s):
        return pl.ds(pl.multiple_of(s * share, HD), share)

    w_copy(0).wait()
    attended = vec[0:1, :]
    for d in range(groups):
        attended = attended + dot(ctx[d][...], w[0, rows_of(srcs[d]), :])
    first, n1, r1 = norm(x[...].astype(F32) + attended, vec[1:2, :], vec[2:3, :])
    low = first.astype(BF16)
    outer = vec[3:4, :] + first
    for j in range(parts):
        w_copy(1 + j).wait()
        w_copy(1 + parts + j).wait()
        inner = dot(low, w[1 + j]) + vec[6 + j : 7 + j, :]
        inner_s[j] = inner
        act = 0.5 * inner * (1.0 + jnp.tanh(GELU_A * (inner + GELU_B * inner * inner * inner)))
        act_low = act.astype(BF16)
        act_s[j] = act_low
        outer = outer + dot(act_low, w[1 + parts + j])
    second, n2, r2 = norm(outer, vec[4:5, :], vec[5:6, :])
    out[...] = second.astype(BF16)
    d_second, dgain2, dshift2 = norm_back(cot[...].astype(F32), n2, r2, vec[4:5, :])
    d_outer = d_second.astype(BF16)
    vec_out[...] = jnp.zeros(vec_out.shape, F32)
    vec_out[4:5, :] = dgain2
    vec_out[5:6, :] = dshift2
    vec_out[3:4, :] = jnp.sum(d_outer.astype(F32), 0, keepdims=True)
    d_first = d_second
    for j in range(parts):
        g[1 + parts + j] = dot_tn(act_s[j], d_outer).astype(BF16)
        g_copy(1 + parts + j).start()
        v = inner_s[j]
        t = jnp.tanh(GELU_A * (v + GELU_B * v * v * v))
        slope = 0.5 * (1.0 + t) + 0.5 * v * (1.0 - t * t) * (
            GELU_A * (1.0 + 3.0 * GELU_B * v * v)
        )
        d_inner = (dot_nt(d_outer, w[1 + parts + j]) * slope).astype(BF16)
        vec_out[6 + j : 7 + j, :] = jnp.sum(d_inner.astype(F32), 0, keepdims=True)
        g[1 + j] = dot_tn(low, d_inner).astype(BF16)
        g_copy(1 + j).start()
        d_first = d_first + dot_nt(d_inner, w[1 + j])
    d_sum, dgain1, dshift1 = norm_back(d_first, n1, r1, vec[1:2, :])
    dsum_out[...] = d_sum
    d_att = d_sum.astype(BF16)
    vec_out[1:2, :] = dgain1
    vec_out[2:3, :] = dshift1
    vec_out[0:1, :] = jnp.sum(d_att.astype(F32), 0, keepdims=True)
    for d in range(groups):
        g[0, rows_of(srcs[d]), :] = dot_tn(ctx[d][...], d_att).astype(BF16)
        dctx[d][...] = dot_nt(d_att, w[0, rows_of(srcs[d]), :]).astype(BF16)
    g_copy(0).start()
    for j in range(blocks):
        g_copy(j).wait()


def middle(place, x, cot, vec, w, ctx, parts, w_col):
    groups = len(ctx)
    rows, width = x.shape
    blocks = 1 + 2 * parts

    def kernel(place_ref, *refs):
        middle_kernel(groups, parts, w_col, place_ref, *refs)

    result = pl.pallas_call(
        kernel,
        out_shape=(
            jax.ShapeDtypeStruct((rows, width), BF16),
            jax.ShapeDtypeStruct((width, blocks * width), BF16),
            jax.ShapeDtypeStruct((rows, width), F32),
            jax.ShapeDtypeStruct((16, width), F32),
        )
        + tuple(jax.ShapeDtypeStruct(c.shape, BF16) for c in ctx),
        in_specs=[smem_spec(), vmem_spec(), vmem_spec(), vmem_spec(), any_spec()]
        + [vmem_spec()] * groups,
        out_specs=(vmem_spec(), any_spec(), vmem_spec(), vmem_spec()) + (vmem_spec(),) * groups,
        scratch_shapes=[
            pltpu.VMEM((blocks, width, width), BF16),
            pltpu.VMEM((blocks, width, width), BF16),
            pltpu.VMEM((parts, rows, width), F32),
            pltpu.VMEM((parts, rows, width), BF16),
            pltpu.SemaphoreType.DMA((blocks,)),
            pltpu.SemaphoreType.DMA((blocks,)),
        ],
        compiler_params=pltpu.CompilerParams(vmem_limit_bytes=VMEM_BYTES),
        cost_estimate=pl.CostEstimate(
            flops=6 * rows * width * width * blocks,
            bytes_accessed=4 * width * width * blocks,
            transcendentals=2 * rows * width * parts,
        ),
        name="middle",
    )(place, x, cot, vec, w, *ctx)
    return result[0], result[1], result[2], result[3], result[4:]


def project_back_kernel(groups, heads, blocks, place, x, w_hbm, flag, dq, *refs):
    dkv = refs[:blocks]
    dx_out, gw_out, bias_out, w, d_all, sem = refs[blocks:]
    rows = x.shape[1]
    cols = w.shape[1]
    half = heads * WIDE
    copy = pltpu.make_async_copy(
        w_hbm.at[:, pl.ds(pl.multiple_of(place[0] * cols, 128), cols)], w, sem
    )
    copy.start()
    for g in range(groups):
        entity = flag[g]
        at = slice(g * rows, (g + 1) * rows)
        for h in range(heads):
            d = dq[h, g].astype(F32)
            d_all[at, h * WIDE : (h + 1) * WIDE] = (d * (1.0 - entity)).astype(BF16)
            d_all[at, half + h * WIDE : half + (h + 1) * WIDE] = (d * entity).astype(BF16)
            total = dkv[0][h, g].astype(F32)
            for p in range(1, blocks):
                total = total + dkv[p][h, g].astype(F32)
            d_all[at, 2 * half + h * WIDE : 2 * half + (h + 1) * WIDE] = total.astype(BF16)
    bias_out[...] = jnp.broadcast_to(
        jnp.sum(d_all[...].astype(F32), 0, keepdims=True), bias_out.shape
    )
    copy.wait()
    for g in range(groups):
        at = slice(g * rows, (g + 1) * rows)
        dx_out[g] = dot_nt(d_all[at, :], w[...]).astype(BF16)
    xs = jnp.concatenate([x[g] for g in range(groups)], 0)
    gw_out[...] = dot_tn(xs, d_all[...]).astype(BF16)


def project_back(place, x, w, flag, dq, dkv, cols):
    groups, rows, width = x.shape
    heads = dq.shape[0]
    blocks = len(dkv)

    def kernel(place_ref, *refs):
        project_back_kernel(groups, heads, blocks, place_ref, *refs)

    return pl.pallas_call(
        kernel,
        out_shape=(
            jax.ShapeDtypeStruct((groups, rows, width), BF16),
            jax.ShapeDtypeStruct((width, cols), BF16),
            jax.ShapeDtypeStruct((8, cols), F32),
        ),
        in_specs=[smem_spec(), vmem_spec(), any_spec(), vmem_spec(), vmem_spec()]
        + [vmem_spec()] * blocks,
        out_specs=(vmem_spec(), vmem_spec(), vmem_spec()),
        scratch_shapes=[
            pltpu.VMEM((width, cols), BF16),
            pltpu.VMEM((groups * rows, cols), BF16),
            pltpu.SemaphoreType.DMA,
        ],
        compiler_params=pltpu.CompilerParams(vmem_limit_bytes=VMEM_BYTES),
        cost_estimate=pl.CostEstimate(
            flops=4 * groups * rows * width * cols, bytes_accessed=4 * width * cols, transcendentals=0
        ),
        name="project_back",
    )(place, x, w, flag, dq, *dkv)


def make_body(groups, cycle):
    blocks = cycle // 2
    heads = HEADS // groups

    def swap_core(v):
        return lax.ppermute(v, "blk", [(i, i ^ 1) for i in range(cycle)])

    def to_block(v, p):
        return lax.ppermute(v, "blk", [(i, i ^ (2 * p)) for i in range(cycle)])

    def shift(v, d):
        return lax.ppermute(v, "head", [(i, (i + d) % groups) for i in range(groups)])

    def total(v):
        bit = 1
        while bit < cycle:
            v = v + lax.ppermute(v, "blk", [(i, i ^ bit) for i in range(cycle)])
            bit *= 2
        bit = 1
        while bit < groups:
            v = v + lax.ppermute(v, "head", [(i, i ^ bit) for i in range(groups)])
            bit *= 2
        return v

    def pick(v, i):
        return lax.dynamic_index_in_dim(v, i, 0, keepdims=False)

    def body(
        hidden,
        entity_flags,
        doc_lengths,
        cotangent,
        query_weight,
        query_bias,
        keyval_weight,
        value_bias,
        output_weight,
        output_bias,
        first_gain,
        first_shift,
        inner_weight,
        inner_bias,
        outer_weight,
        outer_bias,
        second_gain,
        second_shift,
    ):
        micro, own_rows, width = hidden.shape
        hidden_units = inner_bias.shape[0]
        parts = hidden_units // width
        length = own_rows * groups * cycle
        rows = 2 * own_rows
        z = lax.axis_index("head")
        b = lax.axis_index("blk")
        core = lax.rem(b, 2)
        column = b // 2
        place = jnp.stack([z, column, core, b]).astype(jnp.int32)
        everywhere = ("head", "blk")

        both = jnp.stack([hidden, cotangent], 1)
        mine = pick(both, core)
        came = swap_core(pick(both, 1 - core))
        chip = jnp.where(
            core == 0, jnp.concatenate([mine, came], 1), jnp.concatenate([came, mine], 1)
        )
        x = chip[0]
        cot = chip[1]
        xs = [x] + [shift(x, d) for d in range(1, groups)]

        depth = query_weight.shape[0] // (4 * width)
        wq = query_weight.reshape(depth, 2, 2, groups, heads, HD)
        wq = wq.transpose(0, 3, 1, 4, 2, 5).reshape(depth, groups, 4 * heads * HD)
        wkv = keyval_weight.reshape(depth, 2, groups, heads, HD)
        wkv = wkv.transpose(0, 2, 3, 1, 4).reshape(depth, groups, 2 * heads * HD)
        cols = 6 * heads * HD
        w_qkv = jnp.concatenate([wq, wkv], 2).reshape(depth, groups * cols)
        w_in = inner_weight.reshape(depth, width, parts).transpose(0, 2, 1).reshape(depth, hidden_units)
        w_own = jnp.concatenate(
            [
                w_qkv,
                output_weight.reshape(depth, width),
                w_in,
                outer_weight.reshape(depth, hidden_units),
            ],
            1,
        )
        w_all = lax.all_gather(w_own, everywhere, axis=0, tiled=True)

        flags = pick(lax.all_gather(entity_flags, everywhere, axis=1, tiled=True), core)
        lengths = pick(doc_lengths, core)
        count = lengths.shape[0]
        index = jnp.arange(count, dtype=jnp.int32)
        ends = jnp.sum(jnp.where(index[None, :] <= index[:, None], lengths[None, :], 0), 1)
        positions = jnp.arange(length, dtype=jnp.int32)
        docs = jnp.sum((ends[None, :] <= positions[:, None]).astype(jnp.int32), 1)
        docs_seg = docs.reshape(groups, blocks, rows)
        doc_q = lax.dynamic_index_in_dim(docs_seg, column, 1, keepdims=False)
        flag_q = lax.dynamic_index_in_dim(
            flags.reshape(groups, blocks, rows), column, 1, keepdims=False
        ).astype(F32)[..., None]
        code_k = (2 * docs + flags).astype(BF16)[:, None]
        chunk = chunk_of(length)
        firsts = doc_q[:, 0]
        lasts = doc_q[:, rows - 1]
        begin = jnp.sum(jnp.where(index[None, :] < firsts[:, None], lengths[None, :], 0), 1)
        end = jnp.sum(jnp.where(index[None, :] <= lasts[:, None], lengths[None, :], 0), 1)
        span = jnp.stack([begin // chunk, (end + chunk - 1) // chunk], 1).astype(jnp.int32)

        bq = query_bias.astype(F32).reshape(2, 2, groups, heads, HD)
        bq = bq.transpose(2, 0, 3, 1, 4).reshape(groups, 4 * heads * HD)
        bv = value_bias.astype(F32).reshape(groups, heads, 1, HD)
        bv = jnp.concatenate([jnp.zeros_like(bv), bv], 2).reshape(groups, 2 * heads * HD)
        bias = lax.dynamic_slice_in_dim(jnp.concatenate([bq, bv], 1), z, 1, 0)
        q, kv, x_seg = project(place, xs, w_all, bias, flag_q, heads)
        pieces = [kv] + [to_block(kv, p) for p in range(1, blocks)]
        ctx, lse, kv_all, wk_all = attend(place, span, q, pieces, code_k, doc_q.astype(F32))

        ctx_in = [pick(ctx, z)] + [
            shift(pick(ctx, lax.rem(z + d, groups)), d) for d in range(1, groups)
        ]

        vec = jnp.concatenate(
            [
                v.astype(F32).reshape(-1, width)
                for v in (
                    output_bias,
                    first_gain,
                    first_shift,
                    outer_bias,
                    second_gain,
                    second_shift,
                    inner_bias.reshape(width, parts).T,
                )
            ],
            0,
        )
        low_out, g_mid, d_sum, g_vec, d_ctx = middle(
            place, x, cot, vec, w_all, ctx_in, parts, groups * cols
        )
        mid_own = lax.psum_scatter(g_mid, everywhere, scatter_dimension=0, tiled=True).astype(F32)
        vec_sum = total(g_vec)

        d_heads = [d_ctx[0]] + [shift(d_ctx[d], groups - d) for d in range(1, groups)]
        d_heads = [d_heads[0]] + [d_heads[groups - d] for d in range(1, groups)]
        dq, dkv = attend_back(
            place, span, q, kv_all, wk_all, ctx, lse, code_k, doc_q.astype(F32), d_heads
        )
        dkv_in = [dkv[0]] + [to_block(dkv[p], p) for p in range(1, blocks)]
        dx, gw, g_bias = project_back(place, x_seg, w_all, flag_q, dq, dkv_in, cols)

        dx_in = [pick(dx, z)] + [
            shift(pick(dx, lax.rem(z + d, groups)), d) for d in range(1, groups)
        ]
        grad_x = d_sum
        for piece in dx_in:
            grad_x = grad_x + piece.astype(F32)

        halves_g = grad_x.reshape(2, own_rows, width)
        halves_o = low_out.reshape(2, own_rows, width)
        keep_g, send_g = pick(halves_g, core), pick(halves_g, 1 - core)
        keep_o, send_o = pick(halves_o, core), pick(halves_o, 1 - core)
        came_g, came_o = swap_core(send_g), swap_core(send_o)

        def in_order(kept, arrived):
            return jnp.where(core == 0, jnp.stack([kept, arrived]), jnp.stack([arrived, kept]))

        grad_hidden = in_order(keep_g, came_g)
        layer_output = in_order(keep_o, came_o)

        gw = gw.reshape(groups, cycle, depth, cols).transpose(1, 0, 2, 3)
        gw = lax.psum_scatter(gw, "blk", scatter_dimension=0, tiled=True)[0]
        gw = lax.all_to_all(gw, "head", split_axis=0, concat_axis=0, tiled=True).astype(F32)
        grad_query = (
            gw[:, :, : 4 * heads * HD]
            .reshape(groups, depth, 2, heads, 2, HD)
            .transpose(1, 2, 4, 0, 3, 5)
            .reshape(-1)
        )
        grad_keyval = (
            gw[:, :, 4 * heads * HD :]
            .reshape(groups, depth, heads, 2, HD)
            .transpose(1, 3, 0, 2, 4)
            .reshape(-1)
        )
        slot = jnp.arange(groups)[:, None] == z
        bias_sum = total(jnp.where(slot, g_bias[:1], 0.0))
        grad_qbias = (
            bias_sum[:, : 4 * heads * HD]
            .reshape(groups, 2, heads, 2, HD)
            .transpose(1, 3, 0, 2, 4)
            .reshape(4, width)
        )
        grad_vbias = bias_sum[:, 4 * heads * HD :].reshape(groups, heads, 2, HD)[:, :, 1].reshape(width)

        grad_output = mid_own[:, :width].reshape(-1)
        grad_inner = (
            mid_own[:, width : width + hidden_units]
            .reshape(depth, parts, width)
            .transpose(0, 2, 1)
            .reshape(-1)
        )
        grad_outer = mid_own[:, width + hidden_units :].reshape(-1)
        return (
            layer_output,
            grad_hidden,
            grad_query,
            grad_qbias,
            grad_keyval,
            grad_vbias,
            grad_output,
            vec_sum[0],
            vec_sum[1],
            vec_sum[2],
            grad_inner,
            vec_sum[6 : 6 + parts].T.reshape(hidden_units),
            grad_outer,
            vec_sum[3],
            vec_sum[4],
            vec_sum[5],
        )

    return body


def solution(mesh):
    split = P(("head", "blk"))
    tokens = P(None, ("head", "blk"), None)
    return jax.shard_map(
        make_body(mesh.shape["head"], mesh.shape["blk"]),
        mesh=mesh,
        in_specs=(
            tokens,
            P(None, ("head", "blk")),
            P(),
            tokens,
            split,
            P(),
            split,
            P(),
            split,
            P(),
            P(),
            P(),
            split,
            P(),
            split,
            P(),
            P(),
            P(),
        ),
        out_specs=(
            tokens,
            tokens,
            split,
            P(),
            split,
            P(),
            split,
            P(),
            P(),
            P(),
            split,
            P(),
            split,
            P(),
            P(),
            P(),
        ),
        check_vma=False,
    )
```

time: 1390 us -> 503 us (0.36)
  waiting for transfers between devices: 704 us -> 285 us
  matrix products: 183 us -> 0 us
  local copies, waits for them, and re-layouts: 194 us -> 58.4 us
  blocking collectives: 169 us -> 43.1 us
  Pallas kernels: 0 us -> 56.2 us
  other arithmetic: 56.6 us -> 7.56 us
    unnamed x11 -> x3, waiting for transfers between devices: 470 us -> 0.69 us
    dot_general x142 -> x0, matrix products: 183 us -> none  [the longest x16 24.3 us: key_advance(): jnp.einsum('hkq,qhd->khd', d_scores, query_block, preferred_element_type=...]
    all_gather x9 -> x1, waiting for transfers between devices: 223 us -> 59.9 us  [body(): w_all = lax.all_gather(w_own, everywhere, axis=0, tiled=True)]
    reduce_scatter x0 -> x2, waiting for transfers between devices: none -> 132 us  [the longest x1 132 us: body(): lax.psum_scatter(g_mid, everywhere, scatter_dimension=0, tiled=True)]
    ppermute x0 -> x31, waiting for transfers between devices: none -> 87.7 us  [the longest x12 36.6 us: shift(): lax.ppermute(v, 'head', [(i, (i + d) % groups) for i in range(groups)])]
    all_gather x11 -> x1, blocking collectives: 104 us -> 43.1 us  [body(): lax.all_gather(entity_flags, everywhere, axis=1, tiled=True)]
    pallas_call x0 -> x5, Pallas kernels: none -> 56.2 us  [the longest x1 15.3 us: attend_back(): pl.pallas_call(kernel, out_shape=(jax.ShapeDtypeStruct((heads, groups, ro...]
    all_to_all x10 -> x1, starting transfers between devices: 48 us -> 3.65 us  [body(): lax.all_to_all(gw, 'head', split_axis=0, concat_axis=0, tiled=True)]
  transfers between devices with their start and end apart: 20 -> 35, of which waited for: 8 -> 20; matrix products, arithmetic and copies ran while one was open for 29% -> 3% of each run, Pallas kernels for 0% -> 0%
where the time goes in v1:
time: 503 us; the launch traced here: 502 us
  waiting for transfers between devices  285 us (57%)
  local copies, waits for them, and re-layouts  58.4 us (12%)
  Pallas kernels  56.2 us (11%)
  blocking collectives  43.1 us (9%)
  starting transfers between devices  37.3 us (7%)
  between operations  14.5 us (3%)
  other arithmetic  7.56 us (2%)
    reduce_scatter x1, waiting for transfers between devices, body(): lax.psum_scatter(g_mid, everywhere, scatter_dimension=0, tiled=True)  132 us
    all_gather x1, waiting for transfers between devices, body(): w_all = lax.all_gather(w_own, everywhere, axis=0, tiled=True)  59.9 us
    all_gather x1, blocking collectives, body(): lax.all_gather(entity_flags, everywhere, axis=1, tiled=True)  43.1 us
    ppermute x12, waiting for transfers between devices, shift(): lax.ppermute(v, 'head', [(i, (i + d) % groups) for i in range(groups)])  36.6 us
    ppermute x6, waiting for transfers between devices, to_block(): return lax.ppermute(v, 'blk', [(i, i ^ 2 * p) for i in range(cycle)])  32.5 us
    pallas_call x1, Pallas kernels, attend_back(): pl.pallas_call(kernel, out_shape=(jax.ShapeDtypeStruct((heads, groups, ro...  15.3 us
    reshape x3, local copies, waits for them, and re-layouts, body(): grad_inner = mid_own[:, width:width + hidden_units].reshape(depth, parts,...  14.7 us
    pallas_call x1, Pallas kernels, middle(): pl.pallas_call(kernel, out_shape=(jax.ShapeDtypeStruct((rows, width), BF1...  14.3 us
  transfers between devices with their start and end apart: 35, of which 20 were waited for; matrix products, arithmetic and copies ran while one was open for 3% of the time, Pallas kernels for 0%

profile of v1, /device:TPU:0, one launch (start us, length us, event | category | flops | bytes accessed | tf_op | source)
XLA Modules:
  0.0 501.6 jit_solution(2196917173057887235)
XLA Ops:
  12.1 10.9 %reshape.310 = bf16[24,768,4]{2,1,0:T(8,128)(2,1)} reshape(bf16[73728]{0:T(1024)(128)(2,1)S(1)} %copy-done.15) | data formatting | bytes 294912 | tf_op jit(solution)/shard_map/reshape | solution.py:596
  23.0 3.9 copy.117
  29.1 43.1 %all-gather = s32[32,64,2]{1,2,0:T(2,128)S(1)} all-gather(s32[1,64,2]{1,2,0:T(2,128)S(1)} %bitcast.119), channel_id=1, replica_groups=mesh['head'=4,'blk'=8] {'head','blk'}, dimensions={0}, use_global_device_ids=true | all-gather | bytes 16896 | tf_op jit(solution)/shard_map/all_gather | solution.py:608
  77.1 2.0 collective-permute-start.1
  79.7 9.4 %collective-permute-done.3.refs_3_ = bf16[128,768]{1,0:T(8,128)(2,1)S(1)} collective-permute-done((bf16[128,768]{1,0:T(8,128)(2,1)S(1)}, bf16[128,768]{1,0:T(8,128)(2,1)S(1)}, u32[]{:S(2)}, u32[]{:S(2)}) %collective-permute-start.3) | collective-permute-done | bytes 196640 | tf_op jit(solution)/shard_map/ppermute | solution.py:531
  89.0 15.3 %collective-permute-done.2.refs_2_ = bf16[128,768]{1,0:T(8,128)(2,1)S(1)} collective-permute-done((bf16[128,768]{1,0:T(8,128)(2,1)S(1)}, bf16[128,768]{1,0:T(8,128)(2,1)S(1)}, u32[]{:S(2)}, u32[]{:S(2)}) %collective-permute-start.2) | collective-permute-done | bytes 196640 | tf_op jit(solution)/shard_map/ppermute | solution.py:531
  104.4 59.9 %all-gather.3.cloned.1.call-done.refs_4_.refs_3_.refs_1_ = bf16[768,11520]{1,0:T(8,128)(2,1)} async-done(((bf16[24,11520]{1,0:T(8,128)(2,1)}), bf16[768,11520]{1,0:T(8,128)(2,1)}) %all-gather.3.cloned.1.call-update) | async-done | bytes 17694736 | tf_op jit(solution)/shard_map/all_gather | solution.py:606
  164.3 5.1 %project.1 = (bf16[3,4,128,128]{3,2,1,0:T(8,128)(2,1)}, bf16[3,4,128,128]{3,2,1,0:T(8,128)(2,1)}, bf16[4,128,768]{2,1,0:T(8,128)(2,1)}) custom-call(s32[4]{0:T(128)} %pad_add_fusion.1.place_ref, bf16[128,768]{1,0:T(8,128)(2,1)} %copy-done.2, bf16[128,768]{1,0:T(8,128)(2,1)} %copy-done.11, bf16[128,768]{1,0:T(8,128)(2,1)} %copy-done.10, ...), custom_call_target="tpu_custom_call" | custom-call | flops 905969664 | bytes 3538944 | tf_op jit(solution)/shard_map/project/pallas_call | solution.py:77
  169.4 1.5 collective-permute-start.6
  170.9 1.4 collective-permute-start.5
  174.4 8.2 %collective-permute-done.6.refs_3_ = bf16[3,4,128,128]{3,2,1,0:T(8,128)(2,1)S(1)} collective-permute-done((bf16[3,4,128,128]{3,2,1,0:T(8,128)(2,1)}, bf16[3,4,128,128]{3,2,1,0:T(8,128)(2,1)S(1)}, u32[]{:S(2)}, u32[]{:S(2)}) %collective-permute-start.6) | collective-permute-done | bytes 393248 | tf_op jit(solution)/shard_map/ppermute | solution.py:528
  182.6 7.7 %collective-permute-done.5.refs_2_ = bf16[3,4,128,128]{3,2,1,0:T(8,128)(2,1)S(1)} collective-permute-done((bf16[3,4,128,128]{3,2,1,0:T(8,128)(2,1)}, bf16[3,4,128,128]{3,2,1,0:T(8,128)(2,1)S(1)}, u32[]{:S(2)}, u32[]{:S(2)}) %collective-permute-start.5) | collective-permute-done | bytes 393248 | tf_op jit(solution)/shard_map/ppermute | solution.py:528
  191.2 13.5 %attend.1 = (bf16[4,128,192]{2,1,0:T(8,128)(2,1)}, f32[12,128]{1,0:T(8,128)}, bf16[3,2048,128]{2,1,0:T(8,128)(2,1)}, bf16[3,2048,128]{2,1,0:T(8,128)(2,1)}) custom-call(s32[4]{0:T(128)} %pad_add_fusion.1.place_ref, s32[4,2]{1,0:T(4,128)} %pad_add_fusion.span_ref, bf16[3,4,128,128]{3,2,1,0:T(8,128)(2,1)} %get-tuple-element.36.q_ref.refs_0_, ...), custom_call_target="tpu_custom_call" | custom-call | flops 805306368 | bytes 3145728 | tf_op jit(solution)/shard_map/attend/pallas_call | solution.py:186
  204.7 1.6 dynamic-slice_bitcast_fusion.5
  206.3 1.4 collective-permute-start.9
  208.0 1.8 collective-permute-start.7
  211.3 5.0 collective-permute-done.8.refs_6_
  216.9 14.3 %middle.1 = (bf16[128,768]{1,0:T(8,128)(2,1)}, bf16[768,6912]{1,0:T(8,128)(2,1)}, f32[128,768]{1,0:T(8,128)}, f32[16,768]{1,0:T(8,128)}, bf16[128,192]{1,0:T(8,1...) custom-call(s32[4]{0:T(128)} %pad_add_fusion.1.place_ref, ...), custom_call_target="tpu_custom_call" | custom-call | flops 4076863488 | bytes 21233664 | tf_op jit(solution)/shard_map/middle/pallas_call | solution.py:426
  231.3 1.6 collective-permute-start.12
  232.9 2.8 collective-permute-start.13
  235.6 2.6 collective-permute-done.11.refs_8_
  238.2 1.8 collective-permute-done.12.refs_9_
  240.7 15.3 %attend_back.1 = (bf16[3,4,128,128]{3,2,1,0:T(8,128)(2,1)}, bf16[4,3,4,128,128]{4,3,2,1,0:T(8,128)(2,1)}) custom-call(s32[4]{0:T(128)} %pad_add_fusion.1.place_ref, s32[4,2]{1,0:T(4,128)} %pad_add_fusion.span_ref, bf16[3,4,128,128]{3,2,1,0:T(8,128)(2,1)} %get-tuple-element.36.q_ref.refs_0_, bf16[3,2048,128]{2,1,0:T(8,128)(2,1)} %get-tuple-element.42.refs_1_, ...), custom_call_target="tpu_custom_call" | custom-call | flops 2013265920 | bytes 6291456 | tf_op jit(solution)/shard_map/attend_back/pallas_call | solution.py:297
  256.1 2.3 slice_bitcast_fusion
  258.3 1.3 collective-permute-start.16
  259.6 2.2 collective-permute-start.14
  261.8 9.4 %collective-permute-done.16.refs_7_ = bf16[3,4,128,128]{3,2,1,0:T(8,128)(2,1)S(1)} collective-permute-done((bf16[3,4,128,128]{3,2,1,0:T(8,128)(2,1)S(1)}, bf16[3,4,128,128]{3,2,1,0:T(8,128)(2,1)S(1)}, u32[]{:S(2)}, u32[]{:S(2)}) %collective-permute-start.16) | collective-permute-done | bytes 393248 | tf_op jit(solution)/shard_map/ppermute | solution.py:528
  271.3 7.2 %collective-permute-done.15.refs_6_ = bf16[3,4,128,128]{3,2,1,0:T(8,128)(2,1)S(1)} collective-permute-done((bf16[3,4,128,128]{3,2,1,0:T(8,128)(2,1)S(1)}, bf16[3,4,128,128]{3,2,1,0:T(8,128)(2,1)S(1)}, u32[]{:S(2)}, u32[]{:S(2)}) %collective-permute-start.15) | collective-permute-done | bytes 393248 | tf_op jit(solution)/shard_map/ppermute | solution.py:528
  279.3 8.0 %project_back.1 = (bf16[4,128,768]{2,1,0:T(8,128)(2,1)}, bf16[768,1152]{1,0:T(8,128)(2,1)}, f32[8,1152]{1,0:T(8,128)}) custom-call(s32[4]{0:T(128)} %pad_add_fusion.1.place_ref, bf16[4,128,768]{2,1,0:T(8,128)(2,1)} %get-tuple-element.41.refs_0_, bf16[768,11520]{1,0:T(8,128)(2,1)} %all-gather.3.cloned.1.call-done.refs_4_.refs_3_.refs_1_, ...), custom_call_target="tpu_custom_call" | custom-call | flops 1811939328 | bytes 3538944 | tf_op jit(solution)/shard_map/project_back/pallas_call | solution.py:497
  287.3 2.9 copy.143
  291.1 1.2 collective-permute-done.26
  292.6 3.9 collective-permute-done.27
  296.4 1.4 collective-permute-start.28
  297.9 2.7 collective-permute-done.28
  300.6 2.3 collective-permute-start.29
  307.1 2.9 collective-permute-done.30
  310.1 1.2 collective-permute-start.23
  311.3 1.8 collective-permute-start.17
  313.2 2.1 collective-permute-start.19
  315.2 1.2 collective-permute-start.24
  316.4 7.2 %collective-permute-done.24 = f32[4,1152]{1,0:T(4,128)S(1)} collective-permute-done((f32[4,1152]{1,0:T(4,128)S(1)}, f32[4,1152]{1,0:T(4,128)S(1)}, u32[]{:S(2)}, u32[]{:S(2)}) %collective-permute-start.24) | collective-permute-done | bytes 18464 | tf_op jit(solution)/shard_map/ppermute | solution.py:540
  323.7 3.7 collective-permute-start.25
  327.4 2.5 collective-permute-done.18
  330.2 3.7 all-to-all-start
  337.9 4.5 all-to-all-done
  345.3 131.7 %reduce-scatter.5.cloned.1.call-done = bf16[24,6912]{1,0:T(8,128)(2,1)} async-done(((bf16[768,6912]{1,0:T(8,128)(2,1)}), bf16[24,6912]{1,0:T(8,128)(2,1)}) %reduce-scatter.5.cloned.1.call-update) | async-done | bytes 331792 | tf_op jit(solution)/shard_map/reduce_scatter | solution.py:659
  480.4 5.0 %copy.136 = f32[24,4,768]{1,2,0:T(8,128)} copy(f32[24,4,768]{2,1,0:T(4,128)S(1)} %reshape.330) | data formatting | bytes 589824 | tf_op jit(solution)/shard_map/reshape | solution.py:717
  485.5 9.5 %reshape.331 = f32[73728]{0:T(1024)} reshape(f32[24,768,4]{2,1,0:T(8,128)} %bitcast.89) | data formatting | bytes 589824 | tf_op jit(solution)/shard_map/reshape | solution.py:719
  (207 shorter events, 35.2 us)
Async XLA Ops:
  7.2 65.4 %copy-start = (s32[2,32]{1,0:T(2,128)S(1)}, s32[2,32]{1,0:T(2,128)}, u32[]{:S(2)}) copy-start(s32[2,32]{1,0:T(2,128)} %param.20) | copy-start | bytes 772
  7.2 157.1 %all-gather.3.cloned.1.call-start = ((), (), s32[]{:S(2)}) async-start(), calls=%async_computation.3 | async-start | bytes 18247680 | tf_op jit(solution)/shard_map/all_gather | solution.py:606
  27.9 302.2 %reduce-scatter.3.cloned.1.call-start = ((), (), s32[]{:S(2)}) async-start(), calls=%async_computation.4 | async-start | bytes 1990656 | tf_op jit(solution)/shard_map/reduce_scatter | solution.py:690
  28.2 48.1 %collective-permute-start = (bf16[2,64,768]{2,1,0:T(8,128)(2,1)S(1)}, bf16[2,64,768]{2,1,0:T(8,128)(2,1)S(1)}, u32[]{:S(2)}, u32[]{:S(2)}) collective-permute-start(bf16[2,64,768]{2,1,0:T(8,128)(2,1)S(1)} %get-tuple-element.80), channel_id=1, source_target_pairs={{0,1},{1,0},{2,3},{3,2},{4,5},{5,4},{6,7},{7,6},{8,9},{9,8},{10,11... | collective-permute-start | bytes 589832 | tf_op jit(solution)/shard_map/ppermute | solution.py:525
  77.0 87.2 %copy-start.2 = (bf16[128,768]{1,0:T(8,128)(2,1)}, bf16[128,768]{1,0:T(8,128)(2,1)S(1)}, u32[]{:S(2)}) copy-start(bf16[128,768]{1,0:T(8,128)(2,1)S(1)} %get-tuple-element.78.refs_0_) | copy-start | bytes 589828
  77.0 12.0 %collective-permute-start.3 = (bf16[128,768]{1,0:T(8,128)(2,1)S(1)}, bf16[128,768]{1,0:T(8,128)(2,1)S(1)}, u32[]{:S(2)}, u32[]{:S(2)}) collective-permute-start(bf16[128,768]{1,0:T(8,128)(2,1)S(1)} %get-tuple-element.78.refs_0_), channel_id=1, source_target_pairs={{0,24},{8,0},{16,8},{24,16},{1,25},{9,1},{17,9},{25,17},{2,26},{10... | collective-permute-start | bytes 589832 | tf_op jit(solution)/shard_map/ppermute | solution.py:531
  77.1 27.3 %collective-permute-start.2 = (bf16[128,768]{1,0:T(8,128)(2,1)S(1)}, bf16[128,768]{1,0:T(8,128)(2,1)S(1)}, u32[]{:S(2)}, u32[]{:S(2)}) collective-permute-start(bf16[128,768]{1,0:T(8,128)(2,1)S(1)} %get-tuple-element.78.refs_0_), channel_id=1, source_target_pairs={{0,16},{8,24},{16,0},{24,8},{1,17},{9,25},{17,1},{25,9},{2,18},{10... | collective-permute-start | bytes 589832 | tf_op jit(solution)/shard_map/ppermute | solution.py:531
  77.1 27.3 %collective-permute-start.1 = (bf16[128,768]{1,0:T(8,128)(2,1)S(1)}, bf16[128,768]{1,0:T(8,128)(2,1)S(1)}, u32[]{:S(2)}, u32[]{:S(2)}) collective-permute-start(bf16[128,768]{1,0:T(8,128)(2,1)S(1)} %get-tuple-element.78.refs_0_), channel_id=1, source_target_pairs={{0,8},{8,16},{16,24},{24,0},{1,9},{9,17},{17,25},{25,1},{2,10},{10... | collective-permute-start | bytes 589832 | tf_op jit(solution)/shard_map/ppermute | solution.py:531
  89.0 75.2 %copy-start.9 = (bf16[128,768]{1,0:T(8,128)(2,1)}, bf16[128,768]{1,0:T(8,128)(2,1)S(1)}, u32[]{:S(2)}) copy-start(bf16[128,768]{1,0:T(8,128)(2,1)S(1)} %collective-permute-done.3.refs_3_) | copy-start | bytes 589828
  104.3 59.9 %copy-start.10 = (bf16[128,768]{1,0:T(8,128)(2,1)}, bf16[128,768]{1,0:T(8,128)(2,1)S(1)}, u32[]{:S(2)}) copy-start(bf16[128,768]{1,0:T(8,128)(2,1)S(1)} %collective-permute-done.2.refs_2_) | copy-start | bytes 589828
  104.4 59.9 %copy-start.11 = (bf16[128,768]{1,0:T(8,128)(2,1)}, bf16[128,768]{1,0:T(8,128)(2,1)S(1)}, u32[]{:S(2)}) copy-start(bf16[128,768]{1,0:T(8,128)(2,1)S(1)} %collective-permute-done.1.refs_1_) | copy-start | bytes 589828
  169.4 13.2 %collective-permute-start.6 = (bf16[3,4,128,128]{3,2,1,0:T(8,128)(2,1)}, bf16[3,4,128,128]{3,2,1,0:T(8,128)(2,1)S(1)}, u32[]{:S(2)}, u32[]{:S(2)}) collective-permute-start(bf16[3,4,128,128]{3,2,1,0:T(8,128)(2,1)} %get-tuple-element.37.refs_0_), channel_id=1, source_target_pairs={{0,6},{1,7},{2,4},{3,5},{4,2},{5,3},{6,0},{7,1},{8,14},{9,15},{10,... | collective-permute-start | bytes 1179656 | tf_op jit(solution)/shard_map/ppermute | solution.py:528
  170.9 19.3 %collective-permute-start.5 = (bf16[3,4,128,128]{3,2,1,0:T(8,128)(2,1)}, bf16[3,4,128,128]{3,2,1,0:T(8,128)(2,1)S(1)}, u32[]{:S(2)}, u32[]{:S(2)}) collective-permute-start(bf16[3,4,128,128]{3,2,1,0:T(8,128)(2,1)} %get-tuple-element.37.refs_0_), channel_id=1, source_target_pairs={{0,4},{1,5},{2,6},{3,7},{4,0},{5,1},{6,2},{7,3},{8,12},{9,13},{10,... | collective-permute-start | bytes 1179656 | tf_op jit(solution)/shard_map/ppermute | solution.py:528
  172.3 18.0 %collective-permute-start.4 = (bf16[3,4,128,128]{3,2,1,0:T(8,128)(2,1)}, bf16[3,4,128,128]{3,2,1,0:T(8,128)(2,1)S(1)}, u32[]{:S(2)}, u32[]{:S(2)}) collective-permute-start(bf16[3,4,128,128]{3,2,1,0:T(8,128)(2,1)} %get-tuple-element.37.refs_0_), channel_id=1, source_target_pairs={{0,2},{1,3},{2,0},{3,1},{4,6},{5,7},{6,4},{7,5},{8,10},{9,11},{10,... | collective-permute-start | bytes 1179656 | tf_op jit(solution)/shard_map/ppermute | solution.py:528
  191.2 18.7 %copy-start.23 = (bf16[768]{0:T(1024)(128)(2,1)S(1)}, bf16[768]{0:T(1024)(128)(2,1)}, u32[]{:S(2)}) copy-start(bf16[768]{0:T(1024)(128)(2,1)} %param.28) | copy-start | bytes 4612
  191.2 18.7 %copy-start.24 = (bf16[768]{0:T(1024)(128)(2,1)S(1)}, bf16[768]{0:T(1024)(128)(2,1)}, u32[]{:S(2)}) copy-start(bf16[768]{0:T(1024)(128)(2,1)} %param.29) | copy-start | bytes 4612
  191.2 18.7 %copy-start.25 = (bf16[768]{0:T(1024)(128)(2,1)S(1)}, bf16[768]{0:T(1024)(128)(2,1)}, u32[]{:S(2)}) copy-start(bf16[768]{0:T(1024)(128)(2,1)} %param.33) | copy-start | bytes 4612
  191.2 18.7 %copy-start.26 = (bf16[768]{0:T(1024)(128)(2,1)S(1)}, bf16[768]{0:T(1024)(128)(2,1)}, u32[]{:S(2)}) copy-start(bf16[768]{0:T(1024)(128)(2,1)} %param.34) | copy-start | bytes 4612
  191.2 18.7 %copy-start.27 = (bf16[768]{0:T(1024)(128)(2,1)S(1)}, bf16[768]{0:T(1024)(128)(2,1)}, u32[]{:S(2)}) copy-start(bf16[768]{0:T(1024)(128)(2,1)} %param.35) | copy-start | bytes 4612
  191.2 18.7 %copy-start.20 = (bf16[3072]{0:T(1024)(128)(2,1)S(1)}, bf16[3072]{0:T(1024)(128)(2,1)}, u32[]{:S(2)}) copy-start(bf16[3072]{0:T(1024)(128)(2,1)} %param.31) | copy-start | bytes 18436
  206.3 5.0 %collective-permute-start.9 = (bf16[128,192]{1,0:T(8,128)(2,1)S(1)}, bf16[128,192]{1,0:T(8,128)(2,1)S(1)}, u32[]{:S(2)}, u32[]{:S(2)}) collective-permute-start(bf16[128,192]{1,0:T(8,128)(2,1)S(1)} %get-tuple-element.81), channel_id=1, source_target_pairs={{0,24},{8,0},{16,8},{24,16},{1,25},{9,1},{17,9},{25,17},{2,26},{10... | collective-permute-start | bytes 147464 | tf_op jit(solution)/shard_map/ppermute | solution.py:531
  207.7 8.5 %collective-permute-start.8 = (bf16[128,192]{1,0:T(8,128)(2,1)S(1)}, bf16[128,192]{1,0:T(8,128)(2,1)S(1)}, u32[]{:S(2)}, u32[]{:S(2)}) collective-permute-start(bf16[128,192]{1,0:T(8,128)(2,1)S(1)} %get-tuple-element.82), channel_id=1, source_target_pairs={{0,16},{8,24},{16,0},{24,8},{1,17},{9,25},{17,1},{25,9},{2,18},{10... | collective-permute-start | bytes 147464 | tf_op jit(solution)/shard_map/ppermute | solution.py:531
  208.0 8.2 %collective-permute-start.7 = (bf16[128,192]{1,0:T(8,128)(2,1)S(1)}, bf16[128,192]{1,0:T(8,128)(2,1)S(1)}, u32[]{:S(2)}, u32[]{:S(2)}) collective-permute-start(bf16[128,192]{1,0:T(8,128)(2,1)S(1)} %get-tuple-element.83), channel_id=1, source_target_pairs={{0,8},{8,16},{16,24},{24,0},{1,9},{9,17},{17,25},{25,1},{2,10},{10... | collective-permute-start | bytes 147464 | tf_op jit(solution)/shard_map/ppermute | solution.py:531
  231.2 7.0 %collective-permute-start.11 = (bf16[128,192]{1,0:T(8,128)(2,1)}, bf16[128,192]{1,0:T(8,128)(2,1)S(1)}, u32[]{:S(2)}, u32[]{:S(2)}) collective-permute-start(bf16[128,192]{1,0:T(8,128)(2,1)} %get-tuple-element.46), channel_id=1, source_target_pairs={{0,8},{8,16},{16,24},{24,0},{1,9},{9,17},{17,25},{25,1},{2,10},{10... | collective-permute-start | bytes 147464 | tf_op jit(solution)/shard_map/ppermute | solution.py:531
  231.3 8.8 %collective-permute-start.12 = (bf16[128,192]{1,0:T(8,128)(2,1)}, bf16[128,192]{1,0:T(8,128)(2,1)S(1)}, u32[]{:S(2)}, u32[]{:S(2)}) collective-permute-start(bf16[128,192]{1,0:T(8,128)(2,1)} %get-tuple-element.47), channel_id=1, source_target_pairs={{0,16},{8,24},{16,0},{24,8},{1,17},{9,25},{17,1},{25,9},{2,18},{10... | collective-permute-start | bytes 147464 | tf_op jit(solution)/shard_map/ppermute | solution.py:531
  232.9 7.2 %collective-permute-start.13 = (bf16[128,192]{1,0:T(8,128)(2,1)}, bf16[128,192]{1,0:T(8,128)(2,1)S(1)}, u32[]{:S(2)}, u32[]{:S(2)}) collective-permute-start(bf16[128,192]{1,0:T(8,128)(2,1)} %get-tuple-element.48), channel_id=1, source_target_pairs={{0,24},{8,0},{16,8},{24,16},{1,25},{9,1},{17,9},{25,17},{2,26},{10... | collective-permute-start | bytes 147464 | tf_op jit(solution)/shard_map/ppermute | solution.py:531
  258.3 12.9 %collective-permute-start.16 = (bf16[3,4,128,128]{3,2,1,0:T(8,128)(2,1)S(1)}, bf16[3,4,128,128]{3,2,1,0:T(8,128)(2,1)S(1)}, u32[]{:S(2)}, u32[]{:S(2)}) collective-permute-start(bf16[3,4,128,128]{3,2,1,0:T(8,128)(2,1)S(1)} %get-tuple-element.66), channel_id=1, source_target_pairs={{0,6},{1,7},{2,4},{3,5},{4,2},{5,3},{6,0},{7,1},{8,14},{9,15},{10,... | collective-permute-start | bytes 1179656 | tf_op jit(solution)/shard_map/ppermute | solution.py:528
  259.6 18.8 %collective-permute-start.15 = (bf16[3,4,128,128]{3,2,1,0:T(8,128)(2,1)S(1)}, bf16[3,4,128,128]{3,2,1,0:T(8,128)(2,1)S(1)}, u32[]{:S(2)}, u32[]{:S(2)}) collective-permute-start(bf16[3,4,128,128]{3,2,1,0:T(8,128)(2,1)S(1)} %get-tuple-element.67), channel_id=1, source_target_pairs={{0,4},{1,5},{2,6},{3,7},{4,0},{5,1},{6,2},{7,3},{8,12},{9,13},{10,... | collective-permute-start | bytes 1179656 | tf_op jit(solution)/shard_map/ppermute | solution.py:528
  259.6 18.8 %collective-permute-start.14 = (bf16[3,4,128,128]{3,2,1,0:T(8,128)(2,1)S(1)}, bf16[3,4,128,128]{3,2,1,0:T(8,128)(2,1)S(1)}, u32[]{:S(2)}, u32[]{:S(2)}) collective-permute-start(bf16[3,4,128,128]{3,2,1,0:T(8,128)(2,1)S(1)} %get-tuple-element.68), channel_id=1, source_target_pairs={{0,2},{1,3},{2,0},{3,1},{4,6},{5,7},{6,4},{7,5},{8,10},{9,11},{10,... | collective-permute-start | bytes 1179656 | tf_op jit(solution)/shard_map/ppermute | solution.py:528
  290.2 186.8 %reduce-scatter.5.cloned.1.call-start = ((), (), s32[]{:S(2)}) async-start(), calls=%async_computation.5 | async-start | bytes 10948608 | tf_op jit(solution)/shard_map/reduce_scatter | solution.py:659
  290.9 20.4 %copy-start.4 = (bf16[4,128,768]{2,1,0:T(8,128)(2,1)S(1)}, bf16[4,128,768]{2,1,0:T(8,128)(2,1)}, u32[]{:S(2)}) copy-start(bf16[4,128,768]{2,1,0:T(8,128)(2,1)} %get-tuple-element.51) | copy-start | bytes 2359300
  290.9 38.9 %copy-start.5 = (f32[128,768]{1,0:T(8,128)S(1)}, f32[128,768]{1,0:T(8,128)}, u32[]{:S(2)}) copy-start(f32[128,768]{1,0:T(8,128)} %get-tuple-element.40) | copy-start | bytes 1179652
  291.1 1.2 collective-permute-start.26
  292.3 4.1 collective-permute-start.27
  296.4 4.2 collective-permute-start.28
  300.6 4.4 collective-permute-start.29
  303.8 2.4 collective-permute-start.21
  303.8 2.6 collective-permute-start.10
  305.0 5.0 %collective-permute-start.30 = (f32[16,768]{1,0:T(8,128)S(1)}, f32[16,768]{1,0:T(8,128)S(1)}, u32[]{:S(2)}, u32[]{:S(2)}) collective-permute-start(f32[16,768]{1,0:T(8,128)S(1)} %add.165), channel_id=1, source_target_pairs={{0,16},{8,24},{16,0},{24,8},{1,17},{9,25},{17,1},{25,9},{2,18},{10... | collective-permute-start | bytes 147464 | tf_op jit(solution)/shard_map/ppermute | solution.py:540
  306.2 3.8 collective-permute-start.22
  310.1 5.1 %collective-permute-start.23 = (f32[4,1152]{1,0:T(4,128)S(1)}, f32[4,1152]{1,0:T(4,128)S(1)}, u32[]{:S(2)}, u32[]{:S(2)}) collective-permute-start(f32[4,1152]{1,0:T(4,128)S(1)} %fusion.16), channel_id=1, source_target_pairs={{0,4},{1,5},{2,6},{3,7},{4,0},{5,1},{6,2},{7,3},{8,12},{9,13},{10,... | collective-permute-start | bytes 55304 | tf_op jit(solution)/shard_map/ppermute | solution.py:536
  311.3 16.0 %collective-permute-start.17 = (bf16[128,768]{1,0:T(8,128)(2,1)S(1)}, bf16[128,768]{1,0:T(8,128)(2,1)S(1)}, u32[]{:S(2)}, u32[]{:S(2)}) collective-permute-start(bf16[128,768]{1,0:T(8,128)(2,1)S(1)} %get-tuple-element.72), channel_id=1, source_target_pairs={{0,8},{8,16},{16,24},{24,0},{1,9},{9,17},{17,25},{25,1},{2,10},{10... | collective-permute-start | bytes 589832 | tf_op jit(solution)/shard_map/ppermute | solution.py:531
  313.2 14.2 %collective-permute-start.19 = (bf16[128,768]{1,0:T(8,128)(2,1)S(1)}, bf16[128,768]{1,0:T(8,128)(2,1)S(1)}, u32[]{:S(2)}, u32[]{:S(2)}) collective-permute-start(bf16[128,768]{1,0:T(8,128)(2,1)S(1)} %get-tuple-element.73), channel_id=1, source_target_pairs={{0,24},{8,0},{16,8},{24,16},{1,25},{9,1},{17,9},{25,17},{2,26},{10... | collective-permute-start | bytes 589832 | tf_op jit(solution)/shard_map/ppermute | solution.py:531
  315.2 14.7 %collective-permute-start.18 = (bf16[128,768]{1,0:T(8,128)(2,1)S(1)}, bf16[128,768]{1,0:T(8,128)(2,1)S(1)}, u32[]{:S(2)}, u32[]{:S(2)}) collective-permute-start(bf16[128,768]{1,0:T(8,128)(2,1)S(1)} %get-tuple-element.74), channel_id=1, source_target_pairs={{0,16},{8,24},{16,0},{24,8},{1,17},{9,25},{17,1},{25,9},{2,18},{10... | collective-permute-start | bytes 589832 | tf_op jit(solution)/shard_map/ppermute | solution.py:531
  315.2 8.4 %collective-permute-start.24 = (f32[4,1152]{1,0:T(4,128)S(1)}, f32[4,1152]{1,0:T(4,128)S(1)}, u32[]{:S(2)}, u32[]{:S(2)}) collective-permute-start(f32[4,1152]{1,0:T(4,128)S(1)} %add.159), channel_id=1, source_target_pairs={{0,8},{8,0},{16,24},{24,16},{1,9},{9,1},{17,25},{25,17},{2,10},{10... | collective-permute-start | bytes 55304 | tf_op jit(solution)/shard_map/ppermute | solution.py:540
  323.7 11.8 %collective-permute-start.25 = (f32[4,1152]{1,0:T(4,128)S(1)}, f32[4,1152]{1,0:T(4,128)S(1)}, u32[]{:S(2)}, u32[]{:S(2)}) collective-permute-start(f32[4,1152]{1,0:T(4,128)S(1)} %add.160), channel_id=1, source_target_pairs={{0,16},{8,24},{16,0},{24,8},{1,17},{9,25},{17,1},{25,9},{2,18},{10... | collective-permute-start | bytes 55304 | tf_op jit(solution)/shard_map/ppermute | solution.py:540
  330.0 7.1 %collective-permute-start.20 = (f32[64,768]{1,0:T(8,128)S(1)}, f32[64,768]{1,0:T(8,128)S(1)}, u32[]{:S(2)}, u32[]{:S(2)}) collective-permute-start(f32[64,768]{1,0:T(8,128)S(1)} %get-tuple-element.76), channel_id=1, source_target_pairs={{0,1},{1,0},{2,3},{3,2},{4,5},{5,4},{6,7},{7,6},{8,9},{9,8},{10,11... | collective-permute-start | bytes 589832 | tf_op jit(solution)/shard_map/ppermute | solution.py:525
  330.2 12.3 %all-to-all-start = ((bf16[4,24,1152]{2,1,0:T(8,128)(2,1)}), bf16[4,24,1152]{2,1,0:T(8,128)(2,1)S(1)}, u32[]{:S(2)}, u32[]{:S(2)}) async-start(bf16[4,24,1152]{2,1,0:T(8,128)(2,1)} %bitcast.103), calls=%async_computation.1 | async-start | bytes 442368 | tf_op jit(solution)/shard_map/all_to_all | solution.py:691
  (23 other events, 82.6 us)
Sparse Core Ops, SparseCore 0:
  28.1 136.1 all-gather.2
  290.3 38.6 reduce-scatter.2
  335.1 141.8 reduce-scatter.4
